TPU v7x, 32 devices: a whole 2x2x4 slice. The times are simulated.
32 devices in a mesh: dp: 4 (over y, x), graph: 8 (over z, core).
Axes of the slice: x: 2, y: 2, z: 4, core: 2. Of those that a mesh axis runs over, the one named last changes fastest.
Arguments:
- edge_state: bfloat16 [4, 16384, 512], P('dp', 'graph'), may hold values from -6 to 6
- cotangent: bfloat16 [4, 16384, 512], P('dp', 'graph'), may hold values from -6 to 6
- edge_count: int32 [4, 8], P('dp', 'graph'), may hold values from 1024 to 2048, as said below
- triplet_basis: bfloat16 [4, 16, 65536], P('dp', None, 'graph'), may hold values from -6 to 6
- triplet_in: int32 [4, 65536], P('dp', 'graph'), may hold values from 0 to 2047, as said below
- triplet_out: int32 [4, 65536], P('dp', 'graph'), may hold values from 0 to 2047, as said below
- down_weight: bfloat16 [512, 64], replicated, may hold values from -0.25 to 0.25
- basis_weight: bfloat16 [16, 64], replicated, may hold values from -1.5 to 1.5
- bilinear_weight: bfloat16 [64, 64], replicated, may hold values from -0.75 to 0.75
- up_weight: bfloat16 [64, 512], replicated, may hold values from -0.75 to 0.75
- first_weight: bfloat16 [512, 512], replicated, may hold values from -0.25 to 0.25
- second_weight: bfloat16 [512, 512], replicated, may hold values from -0.25 to 0.25
Outputs:
- edge_grad: bfloat16 [4, 16384, 512], P('dp', 'graph')
- down_grad: float32 [512, 64], replicated
- basis_grad: float32 [16, 64], replicated
- bilinear_grad: float32 [64, 64], replicated
- up_grad: float32 [64, 512], replicated
- first_grad: float32 [512, 512], replicated
- second_grad: float32 [512, 512], replicated
Inputs may be any that keep to these rules, and one draw needn't show every extreme that they name: `edge_count`: every entry is a multiple of 128; in every batch some shard holds all 2048 slots live. Slot s * 8192 + j * 1024 + k (s and j below 8, k below 1024) holds a triplet of shard s whose in-edge is row triplet_in of shard j, a live row: below edge_count[b, j]. Slot s * 8192 + t holds a triplet whose out-edge is row triplet_out of shard s, a live row: below edge_count[b, s].
All inputs are finite; a program needn't handle non-finite values.
Results may differ from a plain program's by a relative error of at most 0.0096.
Values may be sent and summed in bfloat16 or wider, within the bound.
No kernel may reach another device: no remote copies, remote signals or barrier semaphores. Data moves between devices by JAX's collectives and lax.ppermute only.
A program may use at most 128 MiB of HBM per device.

v0:
```python
import functools
import math

import jax
import jax.numpy as jnp
from jax import lax
from jax.experimental import pallas as pl
from jax.experimental.pallas import tpu as pltpu
from jax.sharding import PartitionSpec as P

HALF = 0.7071067811865476
F32 = jnp.float32
BF16 = jnp.bfloat16
MIB = 1024 * 1024
FORWARD_GRANT = 10
BACKWARD_GRANT = 10
DENSE_GRANT = 18
FINAL_GRANT = 12


def contract(left, right, left_dim, right_dim):
    return lax.dot_general(
        left, right, (((left_dim,), (right_dim,)), ((), ())), preferred_element_type=F32
    )


def sigmoid(value):
    return 0.5 + 0.5 * jnp.tanh(0.5 * value)


def split_index(index_row, lanes):
    slots = index_row.shape[1]
    low = jnp.bitwise_and(index_row, lanes - 1)
    high = jnp.right_shift(index_row, lanes.bit_length() - 1)
    lane_ids = lax.broadcasted_iota(jnp.int32, (lanes, slots), 0)
    return high, jnp.where(lane_ids == low, 1.0, 0.0).astype(BF16)


def stack(rows, lanes):
    groups = rows.shape[1] // lanes
    return jnp.concatenate([rows[:, g * lanes : (g + 1) * lanes] for g in range(groups)], axis=0)


def unstack(rows, narrow):
    groups = rows.shape[0] // narrow
    return jnp.concatenate([rows[g * narrow : (g + 1) * narrow] for g in range(groups)], axis=1)


def pick_rows(stacked, high, lane_hot, narrow):
    groups = stacked.shape[0] // narrow
    every = contract(stacked, lane_hot, 1, 0)
    picked = jnp.where(high == 0, every[:narrow], 0.0)
    for g in range(1, groups):
        picked = jnp.where(high == g, every[g * narrow : (g + 1) * narrow], picked)
    return picked


def place_rows(values, high, lane_hot, groups):
    zero = jnp.zeros((), values.dtype)
    spread = jnp.concatenate([jnp.where(high == g, values, zero) for g in range(groups)], axis=0)
    return contract(spread.astype(BF16), lane_hot, 1, 1)


def down_kernel(edge_ref, weight_ref, rows_ref, slope_ref):
    lanes = rows_ref.shape[1]
    pre = contract(edge_ref[...], weight_ref[...], 1, 1).T
    logistic = sigmoid(pre)
    rows_ref[...] = stack((pre * logistic).astype(BF16), lanes)
    slope_ref[...] = stack(logistic * (1.0 + pre * (1.0 - logistic)), lanes)


def forward_kernel(shard_ref, rows_ref, *refs):
    rows = rows_ref[...]
    ends, basis, weight_ref = refs[:2], refs[2:4], refs[4]
    totals, fetched_ref, coef_ref = refs[-4:-2], refs[-2], refs[-1]
    shard = shard_ref[0]
    narrow = weight_ref.shape[1]
    groups = totals[0].shape[0] // narrow
    lanes = totals[0].shape[1]
    slots = ends[0].shape[3]
    at = pl.ds(pl.multiple_of(shard * slots, slots), slots)
    for i in range(2):
        high, lane_hot = split_index(ends[i][0, shard], lanes)
        fetched = pick_rows(rows, high, lane_hot, narrow)
        fetched_ref[i] = fetched.astype(BF16)
        coef = contract(weight_ref[...], basis[i][:, at], 0, 0)
        coef_ref[i] = coef.astype(BF16)
        high, lane_hot = split_index(ends[i][1, shard], lanes)
        placed = place_rows(coef * fetched, high, lane_hot, groups)
        if len(refs) == 11:
            placed += refs[5 + i][...]
        totals[i][...] = placed


def dense_kernel(
    count_ref,
    edge_ref,
    cotangent_ref,
    gathered_ref,
    more_ref,
    bilinear_ref,
    up_ref,
    first_ref,
    first_turned_ref,
    second_ref,
    second_turned_ref,
    summed_ref,
    back_ref,
    grads_ref,
    total,
):
    step = pl.program_id(0)
    tile, wide = edge_ref.shape
    narrow = bilinear_ref.shape[0]
    lanes = gathered_ref.shape[1]

    @pl.when(step == 0)
    def _():
        total[...] = jnp.zeros_like(total)

    gathered = unstack((gathered_ref[...] + more_ref[...]).astype(BF16), narrow)
    mixed = contract(bilinear_ref[...], gathered, 0, 0).astype(BF16)
    pre_up = contract(mixed, up_ref[...], 0, 0)
    up_logistic = sigmoid(pre_up)
    summed_half = (edge_ref[...].astype(F32) + pre_up * up_logistic).astype(BF16)
    pre_first = contract(summed_half, first_ref[...], 1, 0)
    first_logistic = sigmoid(pre_first)
    first_rows = (pre_first * first_logistic).astype(BF16)
    pre_second = contract(first_rows, second_ref[...], 1, 0)
    logistic = sigmoid(pre_second)
    row_ids = step * tile + lax.broadcasted_iota(jnp.int32, (tile, 1), 0)
    live = jnp.where(row_ids < count_ref[0, 0], HALF, 0.0)
    back_top = cotangent_ref[...].astype(F32) * live
    back_second = (back_top * (logistic * (1.0 + pre_second * (1.0 - logistic)))).astype(BF16)
    slope = first_logistic * (1.0 + pre_first * (1.0 - first_logistic))
    back_first = (contract(back_second, second_turned_ref[...], 1, 0) * slope).astype(BF16)
    back_summed = back_top + contract(back_first, first_turned_ref[...], 1, 0)
    summed_ref[...] = back_summed.astype(BF16)
    slope = up_logistic * (1.0 + pre_up * (1.0 - up_logistic))
    back_up = (back_summed * slope).astype(BF16)
    back_mixed = contract(back_up, up_ref[...], 1, 1).T.astype(BF16)
    back_ref[...] = stack(contract(bilinear_ref[...], back_mixed, 1, 0).astype(BF16), lanes)
    total[:wide] += contract(summed_half, back_first, 0, 0)
    total[wide : 2 * wide] += contract(first_rows, back_second, 0, 0)
    total[2 * wide : 2 * wide + narrow] += contract(mixed, back_up, 1, 0)
    total[2 * wide + narrow :, :narrow] += contract(gathered, back_mixed, 1, 1)

    @pl.when(step == pl.num_programs(0) - 1)
    def _():
        grads_ref[...] = total[...].astype(BF16)


def backward_kernel(count, shards_ref, own_ref, sibling_ref, *refs):
    fetched, coefs, ends = refs[:count], refs[count : 2 * count], refs[2 * count : 2 * count + 2]
    parts, back_coefs = refs[2 * count + 2 : 3 * count + 2], refs[3 * count + 2 :]
    narrow = fetched[0].shape[1]
    groups = own_ref.shape[0] // narrow
    lanes = own_ref.shape[1]
    for s in range(count):
        shard = shards_ref[s]
        part = None
        for i, back_ref in enumerate((own_ref, sibling_ref)):
            high, lane_hot = split_index(ends[i][1, shard], lanes)
            message = pick_rows(back_ref[...], high, lane_hot, narrow)
            back_coefs[s][i] = (message * fetched[s][i].astype(F32)).astype(BF16)
            high, lane_hot = split_index(ends[i][0, shard], lanes)
            placed = place_rows(message * coefs[s][i].astype(F32), high, lane_hot, groups)
            part = placed if part is None else part + placed
        parts[s][...] = part.astype(BF16)


def basis_kernel(shards_ref, *refs):
    back_coefs, basis, grad_ref = refs[:-3], refs[-3:-1], refs[-1]
    slots = back_coefs[0].shape[2]
    grad = jnp.zeros(grad_ref.shape, F32)
    for s, ref in enumerate(back_coefs):
        at = pl.ds(pl.multiple_of(shards_ref[s] * slots, slots), slots)
        for i in range(2):
            grad += contract(ref[i], basis[i][:, at], 1, 1)
    grad_ref[...] = grad


def final_kernel(count, *refs):
    parts = refs[:count]
    slope_ref, edge_ref, summed_ref, weight_ref, basis_ref, edge_grad_ref, grads_ref, total = refs[
        count:
    ]
    step = pl.program_id(0)
    narrow = weight_ref.shape[0]
    basis_width = basis_ref.shape[1]

    @pl.when(step == 0)
    def _():
        total[...] = jnp.zeros_like(total)

    back_down = parts[0][...].astype(F32)
    for part in parts[1:]:
        back_down += part[...].astype(F32)
    back_pre = unstack((back_down * slope_ref[...]).astype(BF16), narrow)
    total[:narrow] += contract(back_pre, edge_ref[...], 1, 0)
    edge_grad_ref[...] = (
        summed_ref[...].astype(F32) + contract(back_pre, weight_ref[...], 0, 0)
    ).astype(BF16)

    @pl.when(step == pl.num_programs(0) - 1)
    def _():
        total[narrow : narrow + basis_width, :narrow] = basis_ref[...].T
        grads_ref[...] = total[...].astype(BF16)


def scale_kernel(scale, source_ref, *outs):
    row = 0
    for out in outs:
        rows, columns = out.shape
        out[...] = source_ref[row : row + rows, :columns].astype(F32) * scale
        row += rows


def call(kernel, grid, in_specs, out_specs, out_shape, flops, transcendentals=0, scratch=(), aliases=None, grant=8):
    def run(*operands):
        size = sum(x.size * x.dtype.itemsize for x in operands)
        size += sum(math.prod(x.shape) * x.dtype.itemsize for x in out_shape)
        return pl.pallas_call(
            kernel,
            grid=grid,
            in_specs=in_specs,
            out_specs=out_specs,
            out_shape=out_shape,
            scratch_shapes=scratch,
            input_output_aliases=aliases or {},
            compiler_params=pltpu.CompilerParams(vmem_limit_bytes=grant * MIB),
            cost_estimate=pl.CostEstimate(
                flops=flops, bytes_accessed=size, transcendentals=transcendentals
            ),
        )(*operands)

    return run


def whole(*shape):
    return pl.BlockSpec(shape, lambda *_: (0,) * len(shape))


SMEM = pl.BlockSpec(memory_space=pltpu.SMEM)


def in_hbm(array):
    return pltpu.with_memory_space_constraint(array, pltpu.HBM)


def shape(dims, dtype):
    return jax.ShapeDtypeStruct(dims, dtype)


def turned(count, size, stride, turn):
    pairs = []
    for g in range(count):
        place = g // stride % size
        pairs.append((g, g + ((place + turn) % size - place) * stride))
    return pairs


class Line:
    cores = 2

    def __init__(self):
        self.size = lax.axis_size("graph")
        self.chips = math.gcd(self.size // self.cores, 4)
        self.span = self.chips * self.cores
        self.groups = self.size // self.span
        me = lax.axis_index("graph")
        self.core = me % self.cores
        self.chip = me // self.cores % self.chips
        self.group = me // self.span

    def send(self, array, moves):
        pairs = [
            (base + one * self.cores + core, base + other * self.cores + core)
            for base in range(0, self.size, self.span)
            for one, other in moves
            for core in range(self.cores)
        ]
        return lax.ppermute(array, "graph", pairs)

    def trade(self, array, bits):
        return self.send(array, [(chip, chip ^ bits) for chip in range(self.chips)])

    def pair(self, array):
        return lax.ppermute(array, "graph", [(g, g ^ 2) for g in range(self.size)])

    def swap(self, array):
        return lax.ppermute(array, "graph", [(g, g ^ 1) for g in range(self.size)])

    def next_group(self, array):
        return lax.ppermute(array, "graph", turned(self.size, self.groups, self.span, -1))

    def last_group(self, array):
        return lax.ppermute(array, "graph", turned(self.size, self.groups, self.span, 1))

    def shard(self, turn, bits):
        group = (self.group + turn) % self.groups
        shard = group * self.span + (self.chip ^ bits) * self.cores + self.core
        return shard.astype(jnp.int32).reshape(1)


def add(*arrays):
    return sum(a.astype(F32) for a in arrays).astype(BF16)


def after(arrays, *others):
    return lax.optimization_barrier((tuple(arrays), others))[0]


def halves(array, place):
    rows = array.shape[0] // 2
    first = place == 0
    return (
        jnp.where(first, array[:rows], array[rows:]),
        jnp.where(first, array[rows:], array[:rows]),
    )


def joined(mine, other, place):
    return jnp.where(
        place == 0, jnp.concatenate([mine, other]), jnp.concatenate([other, mine])
    )


def piece_of(array, size, place):
    rows = array.shape[0] // size
    return lax.dynamic_slice_in_dim(array, place * rows, rows, 0)


def dp_pieces(array):
    size, me = lax.axis_size("dp"), lax.axis_index("dp")
    arrived = [piece_of(array, size, me)]
    for turn in range(1, size):
        away = piece_of(array, size, (me + turn) % size)
        arrived.append(lax.ppermute(away, "dp", turned(size, size, 1, turn)))
    return arrived


def dp_joined(piece):
    size, me = lax.axis_size("dp"), lax.axis_index("dp")
    rows = piece.shape[0]
    out = jnp.zeros((size * rows, piece.shape[1]), piece.dtype)
    out = lax.dynamic_update_slice_in_dim(out, piece, me * rows, 0)
    for turn in range(1, size):
        other = lax.ppermute(piece, "dp", turned(size, size, 1, turn))
        out = lax.dynamic_update_slice_in_dim(out, other, (me - turn) % size * rows, 0)
    return out


def across_chips(array, line):
    mine, away = halves(array, line.chip % 2)
    return [mine, line.pair(away)]


def across_cores(array, line):
    mine, away = halves(array, line.core)
    return [mine, line.swap(away)]


def summed_dp(array):
    size = lax.axis_size("dp")
    for bit in range(size.bit_length() - 1):
        array = add(array, lax.ppermute(array, "dp", [(g, g ^ (1 << bit)) for g in range(size)]))
    return array


def summed_graph(array, line, bits):
    for bit in bits:
        pairs = [(g, g ^ (1 << bit)) for g in range(line.size)]
        array = add(array, lax.ppermute(array, "graph", pairs))
    return array


def local(
    edge_state,
    cotangent,
    edge_count,
    triplet_basis,
    triplet_in,
    triplet_out,
    down_weight,
    basis_weight,
    bilinear_weight,
    up_weight,
    first_weight,
    second_weight,
):
    edge_rows = edge_state[0]
    row_count, wide = edge_rows.shape
    line = Line()
    shards, chips = line.size, line.chips
    narrow = down_weight.shape[1]
    down_weight = down_weight.T
    basis = triplet_basis[0]
    basis_width, tri_rows = basis.shape
    slots = tri_rows // shards
    lanes = math.gcd(row_count, 256)
    stacked = narrow * (row_count // lanes)
    tile = math.gcd(row_count, 512)
    tiles = row_count // tile
    row_spec = pl.BlockSpec((tile, wide), lambda i: (i, 0))
    stack_spec = pl.BlockSpec((narrow * (tile // lanes), lanes), lambda i: (i, 0))
    rows_spec = whole(stacked, lanes)

    ends = jnp.stack([triplet_in.reshape(shards, 1, slots), triplet_out.reshape(shards, 1, slots)])
    triplet_specs = (
        [whole(2, shards, 1, slots)] * 2
        + [whole(basis_width, tri_rows)] * 2
        + [whole(basis_width, narrow)]
    )
    block_flops = 8 * slots * row_count * narrow

    down_rows, down_slope = call(
        down_kernel,
        (tiles,),
        [row_spec, whole(narrow, wide)],
        [stack_spec] * 2,
        [shape((stacked, lanes), BF16), shape((stacked, lanes), F32)],
        2 * row_count * wide * narrow,
        row_count * narrow,
    )(in_hbm(edge_rows), in_hbm(down_weight))

    slot_spec = whole(2, narrow, slots)
    slot_shape = pltpu.HBM((2, narrow, slots), BF16)

    ends, leaving = after((ends, basis), down_rows)
    ends_sibling = line.swap(ends)
    basis_sibling = line.swap(leaving)
    triplets = (ends, ends_sibling, basis, basis_sibling, basis_weight)

    def forward(turn, bits, rows, totals):
        total_shape = shape((stacked, lanes), F32)
        final = line.groups == 1 and bits == chips - 1
        out = call(
            forward_kernel,
            (),
            [SMEM, rows_spec] + triplet_specs + [rows_spec] * len(totals),
            [rows_spec] * 2 + [slot_spec] * 2,
            [pltpu.HBM((stacked, lanes), F32) if final else total_shape, total_shape]
            + [slot_shape] * 2,
            block_flops,
            aliases={7 + i: i for i in range(len(totals)) if i == 1 or not final},
            grant=FORWARD_GRANT,
        )(line.shard(turn, bits), rows, *triplets, *totals)
        return tuple(out[:2]), tuple(out[2:])

    def forward_line(turn, rows, totals, *others):
        arriving = [line.trade(rows, bits) for bits in range(1, chips)]
        totals, got = forward(turn, 0, rows, totals)
        kept = [got]
        for bits in range(1, chips):
            (rows,) = after((arriving[bits - 1],), *totals, *others)
            totals, got = forward(turn, bits, rows, totals)
            kept.append(got)
        return totals, kept

    first_turned, second_turned = after((first_weight, second_weight), down_rows)
    first_turned, second_turned = first_turned.T, second_turned.T
    totals, kept = forward_line(0, down_rows, (), first_turned, second_turned)
    if line.groups > 1:

        def forward_turn(carry, turn):
            rows, totals = carry
            rows = line.next_group(rows)
            totals, got = forward_line(turn, rows, totals)
            return (rows, totals), got

        (_, totals), more_kept = lax.scan(
            forward_turn, (down_rows, totals), jnp.arange(1, line.groups)
        )

    grad_rows = 2 * wide + 2 * narrow
    back_summed, back_gathered, dense_grads = call(
        dense_kernel,
        (tiles,),
        [
            SMEM,
            row_spec,
            row_spec,
            stack_spec,
            stack_spec,
            whole(narrow, narrow),
            whole(narrow, wide),
            whole(wide, wide),
            whole(wide, wide),
            whole(wide, wide),
            whole(wide, wide),
        ],
        [row_spec, stack_spec, whole(grad_rows, wide)],
        [
            pltpu.HBM((row_count, wide), BF16),
            shape((stacked, lanes), BF16),
            shape((grad_rows, wide), BF16),
        ],
        12 * row_count * wide * wide + 6 * row_count * wide * narrow,
        3 * row_count * wide,
        scratch=[pltpu.VMEM((grad_rows, wide), F32)],
        grant=DENSE_GRANT,
    )(
        edge_count,
        in_hbm(edge_rows),
        in_hbm(cotangent[0]),
        in_hbm(totals[0]) if line.groups == 1 else totals[0],
        line.swap(totals[1]),
        bilinear_weight,
        up_weight,
        in_hbm(first_weight),
        first_turned,
        in_hbm(second_weight),
        second_turned,
    )
    back_sibling = line.swap(back_gathered)

    def backward(turn, bits, kept, others=()):
        count = len(bits)
        (back,) = after((back_gathered,), *others)
        out = call(
            functools.partial(backward_kernel, count),
            (),
            [SMEM] + [rows_spec] * 2 + [slot_spec] * (2 * count) + triplet_specs[:2],
            [rows_spec] * count + [slot_spec] * count,
            [shape((stacked, lanes), BF16)] * count + [shape((2, narrow, slots), BF16)] * count,
            count * block_flops,
            grant=BACKWARD_GRANT,
        )(
            jnp.concatenate([line.shard(turn, one) for one in bits]),
            back,
            back_sibling,
            *[kept[one][0] for one in bits],
            *[kept[one][1] for one in bits],
            ends,
            ends_sibling,
        )
        return out[:count], out[count:]

    graph_bits = line.size.bit_length() - 1

    def backward_line(turn, kept, pieces=None):
        parts, others = [], ()
        last_coefs = near_coefs = ()
        if chips == 4:
            (last,), last_coefs = backward(turn, (3,), kept)
            passed = line.send(last, [(0, 1), (3, 2)])
            middle = line.send(last, [(1, 2), (2, 1)])
            others = (last,)
        if pieces is not None:
            pieces = add(*after(pieces, *others))
            others = (*others, pieces)
            arriving = dp_pieces(pieces)
        if chips == 4:
            (near, far), near_coefs = backward(turn, (1, 2), kept, others)
            (passed,) = after((passed,), far)
            if pieces is not None:
                pieces = add(*after(arriving, far))
                (far,) = after((far,), pieces)
            far = add(far, passed)
            (middle,) = after((middle,), far)
            (far,) = after((far,), middle)
            others = (far,)
            parts = [middle, line.trade(far, 2), line.trade(near, 1)]
        elif chips == 2:
            (near,), near_coefs = backward(turn, (1,), kept, others)
            parts = [line.trade(near, 1)]
        (own,), own_coefs = backward(turn, (0,), kept, others)
        if pieces is not None and chips < 4:
            pieces = add(*arriving)
        back_coefs = [*own_coefs, *near_coefs, *last_coefs]
        basis_grad = call(
            basis_kernel,
            (),
            [SMEM] + [slot_spec] * chips + triplet_specs[2:4],
            [whole(narrow, basis_width)],
            [shape((narrow, basis_width), F32)],
            4 * chips * slots * narrow * basis_width,
        )(
            jnp.concatenate([line.shard(turn, bits) for bits in range(chips)]),
            *back_coefs,
            basis,
            basis_sibling,
        )[0]
        return [own] + parts, basis_grad, pieces

    back_parts, basis_grad, dense_grads = backward_line(0, kept, across_cores(dense_grads, line))
    if chips > 1:
        dense_grads = add(*across_chips(dense_grads, line))
    dense_grads = summed_graph(dense_grads, line, range(2, graph_bits))
    if line.groups > 1:

        def backward_turn(carry, one):
            traveling, basis_grad = carry
            turn, got = one
            parts, more, _ = backward_line(turn, got)
            return (line.last_group(add(traveling, *parts)), basis_grad + more), None

        (traveling, basis_grad), _ = lax.scan(
            backward_turn,
            (jnp.zeros((stacked, lanes), BF16), basis_grad),
            (jnp.arange(1, line.groups), more_kept),
            reverse=True,
        )
        back_parts = back_parts + [traveling]

    small_rows = narrow + basis_width
    edge_grad, small_grads = call(
        functools.partial(final_kernel, len(back_parts)),
        (tiles,),
        [stack_spec] * len(back_parts)
        + [stack_spec, row_spec, row_spec, whole(narrow, wide), whole(narrow, basis_width)],
        [row_spec, whole(small_rows, wide)],
        [shape((row_count, wide), BF16), shape((small_rows, wide), BF16)],
        4 * row_count * wide * narrow,
        scratch=[pltpu.VMEM((small_rows, wide), F32)],
        grant=FINAL_GRANT,
    )(
        *back_parts,
        down_slope,
        edge_rows,
        back_summed,
        down_weight,
        basis_grad,
    )

    small_grads = add(*across_cores(small_grads, line))
    small_grads = summed_dp(summed_graph(small_grads, line, range(1, graph_bits)))
    small_grads = joined(small_grads, line.swap(small_grads), line.core)
    if chips > 1:
        dense_grads = joined(dense_grads, line.pair(dense_grads), line.chip % 2)
    dense_grads = dp_joined(dense_grads)
    dense_grads = joined(dense_grads, line.swap(dense_grads), line.core)
    scale = 1.0 / math.sqrt(lax.axis_size("dp") * shards * row_count)

    def scaled(source, *dims):
        return call(
            functools.partial(scale_kernel, scale),
            (),
            [whole(*source.shape)],
            [whole(*d) for d in dims],
            [shape(d, F32) for d in dims],
            source.size,
        )(source)

    first_grad, second_grad, up_grad, bilinear_grad = scaled(
        dense_grads, (wide, wide), (wide, wide), (narrow, wide), (narrow, narrow)
    )
    down_grad, basis_grad = scaled(small_grads, (narrow, wide), (basis_width, narrow))
    return (
        edge_grad[None],
        down_grad.T,
        basis_grad,
        bilinear_grad,
        up_grad,
        first_grad,
        second_grad,
    )


def solution(mesh):
    in_specs = (
        P("dp", "graph", None),
        P("dp", "graph", None),
        P("dp", "graph"),
        P("dp", None, "graph"),
        P("dp", "graph"),
        P("dp", "graph"),
        P(),
        P(),
        P(),
        P(),
        P(),
        P(),
    )
    out_specs = (P("dp", "graph", None), P(), P(), P(), P(), P(), P())
    return jax.shard_map(local, mesh=mesh, in_specs=in_specs, out_specs=out_specs, check_vma=False)
```

profile of v0, /device:TPU:0, one launch (start us, length us, event | category | flops | bytes accessed | tf_op | source)
XLA Modules:
  0.0 119.2 jit_solution(6674198543544190053)
XLA Ops:
  0.7 3.3 %shard_map.171 = (bf16[512,256]{1,0:T(8,128)(2,1)S(1)}, f32[512,256]{1,0:T(8,128)S(1)}) custom-call(bf16[2048,512]{1,0:T(8,128)(2,1)} %bitcast.14, bf16[64,512]{1,0:T(8,128)(2,1)} %bitcast.19), custom_call_target="tpu_custom_call" | custom-call | flops 134217728 | bytes 2949120 | tf_op jit(solution)/shard_map/pallas_call | solution.py:223
  4.6 2.6 %collective-permute-start.2 = (bf16[512,256]{1,0:T(8,128)(2,1)S(1)}, bf16[512,256]{1,0:T(8,128)(2,1)}, u32[]{:S(2)}, u32[]{:S(2)}) collective-permute-start(bf16[512,256]{1,0:T(8,128)(2,1)S(1)} %get-tuple-element.63.rows_ref), channel_id=1, source_target_pairs={{0,2},{1,3},{2,0},{3,1},{4,6},{5,7},{6,4},{7,5},{8,10},{9,11},{10,... | collective-permute-start | bytes 786440 | tf_op jit(solution)/shard_map/ppermute | solution.py:283
  7.4 2.6 %collective-permute-start.1 = (bf16[512,256]{1,0:T(8,128)(2,1)S(1)}, bf16[512,256]{1,0:T(8,128)(2,1)S(1)}, u32[]{:S(2)}, u32[]{:S(2)}) collective-permute-start(bf16[512,256]{1,0:T(8,128)(2,1)S(1)} %get-tuple-element.63.rows_ref), channel_id=1, source_target_pairs={{0,4},{1,5},{2,6},{3,7},{4,0},{5,1},{6,2},{7,3},{8,12},{9,13},{10,... | collective-permute-start | bytes 786440 | tf_op jit(solution)/shard_map/ppermute | solution.py:283
  10.5 2.1 %shard_map.172 = (f32[512,256]{1,0:T(8,128)S(1)}, f32[512,256]{1,0:T(8,128)S(1)}, bf16[2,64,1024]{2,1,0:T(8,128)(2,1)}, bf16[2,64,1024]{2,1,0:T(8,128)(2,1)}) custom-call(s32[1]{0:T(128)} %bitcast.shard_ref.shards_ref, bf16[512,256]{1,0:T(8,128)(2,1)S(1)} %get-tuple-element.63.rows_ref, s32[2,8,1,1024]{3,2,1,0:T(1,128)S(1)} %pad_add_fusion.refs_0_.refs_2_.refs_4_, ...), custom_call_target="tpu_custom_call" | custom-call | flops 1073741824 | bytes 2492420 | tf_op jit(solution)/shard_map/pallas_call | solution.py:223
  12.6 6.7 %collective-permute-done.2.rows_ref = bf16[512,256]{1,0:T(8,128)(2,1)} collective-permute-done((bf16[512,256]{1,0:T(8,128)(2,1)S(1)}, bf16[512,256]{1,0:T(8,128)(2,1)}, u32[]{:S(2)}, u32[]{:S(2)}) %collective-permute-start.2) | collective-permute-done | bytes 262176 | tf_op jit(solution)/shard_map/ppermute | solution.py:283
  19.3 3.1 %shard_map.173 = (f32[512,256]{1,0:T(8,128)S(1)}, f32[512,256]{1,0:T(8,128)S(1)}, bf16[2,64,1024]{2,1,0:T(8,128)(2,1)}, bf16[2,64,1024]{2,1,0:T(8,128)(2,1)}) custom-call(s32[1]{0:T(128)} %bitcast.6.shard_ref, bf16[512,256]{1,0:T(8,128)(2,1)} %collective-permute-done.2.rows_ref, ...), custom_call_target="tpu_custom_call", output_to_operand_aliasing={{0}: (7, {}), {1}: (8, {})} | custom-call | flops 1073741824 | bytes 3540996 | tf_op jit(solution)/shard_map/pallas_call | solution.py:223
  22.4 6.3 %collective-permute-done.1.rows_ref = bf16[512,256]{1,0:T(8,128)(2,1)S(1)} collective-permute-done((bf16[512,256]{1,0:T(8,128)(2,1)S(1)}, bf16[512,256]{1,0:T(8,128)(2,1)S(1)}, u32[]{:S(2)}, u32[]{:S(2)}) %collective-permute-start.1) | collective-permute-done | bytes 262176 | tf_op jit(solution)/shard_map/ppermute | solution.py:283
  28.7 2.1 %shard_map.174 = (f32[512,256]{1,0:T(8,128)S(1)}, f32[512,256]{1,0:T(8,128)S(1)}, bf16[2,64,1024]{2,1,0:T(8,128)(2,1)}, bf16[2,64,1024]{2,1,0:T(8,128)(2,1)}) custom-call(s32[1]{0:T(128)} %bitcast.5.shard_ref, bf16[512,256]{1,0:T(8,128)(2,1)S(1)} %collective-permute-done.1.rows_ref, ...), custom_call_target="tpu_custom_call", output_to_operand_aliasing={{0}: (7, {}), {1}: (8, {})} | custom-call | flops 1073741824 | bytes 3540996 | tf_op jit(solution)/shard_map/pallas_call | solution.py:223
  30.8 2.3 %shard_map.175 = (f32[512,256]{1,0:T(8,128)}, f32[512,256]{1,0:T(8,128)S(1)}, bf16[2,64,1024]{2,1,0:T(8,128)(2,1)}, bf16[2,64,1024]{2,1,0:T(8,128)(2,1)}) custom-call(s32[1]{0:T(128)} %bitcast.3.shard_ref.shards_ref, bf16[512,256]{1,0:T(8,128)(2,1)S(1)} %collective-permute-done.rows_ref, ...), custom_call_target="tpu_custom_call", output_to_operand_aliasing={{1}: (8, {})} | custom-call | flops 1073741824 | bytes 3540996 | tf_op jit(solution)/shard_map/pallas_call | solution.py:223
  35.0 15.1 %shard_map.176 = (bf16[2048,512]{1,0:T(8,128)(2,1)}, bf16[512,256]{1,0:T(8,128)(2,1)S(1)}, bf16[1152,512]{1,0:T(8,128)(2,1)S(1)}) custom-call(s32[1,1]{1,0:T(1,128)S(6)} %copy.35.count_ref, bf16[2048,512]{1,0:T(8,128)(2,1)} %bitcast.15, bf16[2048,512]{1,0:T(8,128)(2,1)} %bitcast.29, f32[512,256]{1,0:T(8,128)} %get-tuple-element.77.gathered_ref, ...), custom_call_target="tpu_custom_call" | custom-call | flops 6845104128 | bytes 10952708 | tf_op jit(solution)/shard_map/pallas_call | solution.py:223
  51.9 1.7 %collective-permute-done.6.sibling_ref = bf16[512,256]{1,0:T(8,128)(2,1)S(1)} collective-permute-done((bf16[512,256]{1,0:T(8,128)(2,1)S(1)}, bf16[512,256]{1,0:T(8,128)(2,1)S(1)}, u32[]{:S(2)}, u32[]{:S(2)}) %collective-permute-start.6) | collective-permute-done | bytes 262176 | tf_op jit(solution)/shard_map/ppermute | solution.py:292
  53.7 2.0 %shard_map.177 = (bf16[512,256]{1,0:T(8,128)(2,1)S(1)}, bf16[2,64,1024]{2,1,0:T(8,128)(2,1)S(1)}) custom-call(s32[1]{0:T(128)} %bitcast.3.shard_ref.shards_ref, bf16[512,256]{1,0:T(8,128)(2,1)S(1)} %get-tuple-element.100.own_ref, bf16[512,256]{1,0:T(8,128)(2,1)S(1)} %collective-permute-done.6.sibling_ref, bf16[2,64,1024]{2,1,0:T(8,128)(2,1)S(1)} %copy-done.11, ...), custom_call_target="tpu_custom_call" | custom-call | flops 1073741824 | bytes 1703940 | tf_op jit(solution)/shard_map/pallas_call | solution.py:223
  55.7 5.4 %collective-permute-start.11 = (bf16[512,256]{1,0:T(8,128)(2,1)S(1)}, bf16[512,256]{1,0:T(8,128)(2,1)S(1)}, u32[]{:S(2)}, u32[]{:S(2)}) collective-permute-start(bf16[512,256]{1,0:T(8,128)(2,1)S(1)} %get-tuple-element.82), channel_id=1, source_target_pairs={{0,2},{1,3},{6,4},{7,5},{8,10},{9,11},{14,12},{15,13},{16,18},{17,... | collective-permute-start | bytes 786440 | tf_op jit(solution)/shard_map/ppermute | solution.py:283
  63.2 1.5 %collective-permute-start.8 = (bf16[144,512]{1,0:T(8,128)(2,1)S(1)}, bf16[144,512]{1,0:T(8,128)(2,1)S(1)}, u32[]{:S(2)}, u32[]{:S(2)}) collective-permute-start(bf16[144,512]{1,0:T(8,128)(2,1)S(1)} %get-tuple-element.125), channel_id=1, source_target_pairs={{0,8},{8,16},{16,24},{24,0},{1,9},{9,17},{17,25},{25,1},{2,10},{10... | collective-permute-start | bytes 442376 | tf_op jit(solution)/shard_map/ppermute | solution.py:339
  64.7 1.5 %collective-permute-start.9 = (bf16[144,512]{1,0:T(8,128)(2,1)S(1)}, bf16[144,512]{1,0:T(8,128)(2,1)S(1)}, u32[]{:S(2)}, u32[]{:S(2)}) collective-permute-start(bf16[144,512]{1,0:T(8,128)(2,1)S(1)} %get-tuple-element.124), channel_id=1, source_target_pairs={{0,16},{8,24},{16,0},{24,8},{1,17},{9,25},{17,1},{25,9},{2,18},{10... | collective-permute-start | bytes 442376 | tf_op jit(solution)/shard_map/ppermute | solution.py:339
  66.3 1.4 %collective-permute-start.10 = (bf16[144,512]{1,0:T(8,128)(2,1)S(1)}, bf16[144,512]{1,0:T(8,128)(2,1)S(1)}, u32[]{:S(2)}, u32[]{:S(2)}) collective-permute-start(bf16[144,512]{1,0:T(8,128)(2,1)S(1)} %get-tuple-element.123), channel_id=1, source_target_pairs={{0,24},{8,0},{16,8},{24,16},{1,25},{9,1},{17,9},{25,17},{2,26},{10... | collective-permute-start | bytes 442376 | tf_op jit(solution)/shard_map/ppermute | solution.py:339
  67.7 3.7 %shard_map.178 = (bf16[512,256]{1,0:T(8,128)(2,1)S(1)}, bf16[512,256]{1,0:T(8,128)(2,1)S(1)}, bf16[2,64,1024]{2,1,0:T(8,128)(2,1)S(1)}, bf16[2,64,1024]{2,1,0:T(8,128)(2,1)S(1)}) custom-call(s32[2]{0:T(128)S(1)} %pad_add_fusion.1.shards_ref, bf16[512,256]{1,0:T(8,128)(2,1)S(1)} %get-tuple-element.100.own_ref, ...), custom_call_target="tpu_custom_call" | custom-call | flops 2147483648 | bytes 2752520 | tf_op jit(solution)/shard_map/pallas_call | solution.py:223
  71.4 2.2 %collective-permute-start.14 = (bf16[512,256]{1,0:T(8,128)(2,1)S(1)}, bf16[512,256]{1,0:T(8,128)(2,1)S(1)}, u32[]{:S(2)}, u32[]{:S(2)}) collective-permute-start(bf16[512,256]{1,0:T(8,128)(2,1)S(1)} %get-tuple-element.104), channel_id=1, source_target_pairs={{0,2},{1,3},{2,0},{3,1},{4,6},{5,7},{6,4},{7,5},{8,10},{9,11},{10,... | collective-permute-start | bytes 786440 | tf_op jit(solution)/shard_map/ppermute | solution.py:283
  73.9 1.5 %collective-permute-start.13 = (bf16[512,256]{1,0:T(8,128)(2,1)S(1)}, bf16[512,256]{1,0:T(8,128)(2,1)S(1)}, u32[]{:S(2)}, u32[]{:S(2)}) collective-permute-start(bf16[512,256]{1,0:T(8,128)(2,1)S(1)} %add_convert_fusion.1), channel_id=1, source_target_pairs={{0,4},{1,5},{2,6},{3,7},{4,0},{5,1},{6,2},{7,3},{8,12},{9,13},{10,... | collective-permute-start | bytes 786440 | tf_op jit(solution)/shard_map/ppermute | solution.py:283
  76.4 2.0 %shard_map.179 = (bf16[512,256]{1,0:T(8,128)(2,1)S(1)}, bf16[2,64,1024]{2,1,0:T(8,128)(2,1)S(1)}) custom-call(s32[1]{0:T(128)} %bitcast.shard_ref.shards_ref, bf16[512,256]{1,0:T(8,128)(2,1)S(1)} %get-tuple-element.100.own_ref, bf16[512,256]{1,0:T(8,128)(2,1)S(1)} %collective-permute-done.6.sibling_ref, bf16[2,64,1024]{2,1,0:T(8,128)(2,1)S(1)} %copy-done.13, ...), custom_call_target="tpu_custom_call" | custom-call | flops 1073741824 | bytes 1703940 | tf_op jit(solution)/shard_map/pallas_call | solution.py:223
  79.4 6.3 %collective-permute-done.21 = bf16[72,512]{1,0:T(8,128)(2,1)S(1)} collective-permute-done((bf16[72,512]{1,0:T(8,128)(2,1)S(1)}, bf16[72,512]{1,0:T(8,128)(2,1)S(1)}, u32[]{:S(2)}, u32[]{:S(2)}) %collective-permute-start.21) | collective-permute-done | bytes 73760 | tf_op jit(solution)/shard_map/ppermute | solution.py:289
  85.7 2.5 %collective-permute-start.22 = (bf16[72,512]{1,0:T(8,128)(2,1)S(1)}, bf16[72,512]{1,0:T(8,128)(2,1)S(1)}, u32[]{:S(2)}, u32[]{:S(2)}) collective-permute-start(bf16[72,512]{1,0:T(8,128)(2,1)S(1)} %add_convert_fusion.4), channel_id=1, source_target_pairs={{0,4},{1,5},{2,6},{3,7},{4,0},{5,1},{6,2},{7,3},{8,12},{9,13},{10,... | collective-permute-start | bytes 221192 | tf_op jit(solution)/shard_map/ppermute | solution.py:374
  88.5 2.8 %shard_map.181 = (bf16[2048,512]{1,0:T(8,128)(2,1)}, bf16[80,512]{1,0:T(8,128)(2,1)S(1)}) custom-call(bf16[512,256]{1,0:T(8,128)(2,1)S(1)} %get-tuple-element.103.refs_0_, bf16[512,256]{1,0:T(8,128)(2,1)S(1)} %collective-permute-done.12.refs_1_, bf16[512,256]{1,0:T(8,128)(2,1)S(1)} %collective-permute-done.13.refs_2_, ...), custom_call_target="tpu_custom_call" | custom-call | flops 268435456 | bytes 8015872 | tf_op jit(solution)/shard_map/pallas_call | solution.py:223
  91.4 2.2 %collective-permute-start.23 = (bf16[72,512]{1,0:T(8,128)(2,1)S(1)}, bf16[72,512]{1,0:T(8,128)(2,1)S(1)}, u32[]{:S(2)}, u32[]{:S(2)}) collective-permute-start(bf16[72,512]{1,0:T(8,128)(2,1)S(1)} %add_convert_fusion.3), channel_id=1, source_target_pairs={{0,2},{1,3},{2,0},{3,1},{4,6},{5,7},{6,4},{7,5},{8,10},{9,11},{10,... | collective-permute-start | bytes 221192 | tf_op jit(solution)/shard_map/ppermute | solution.py:289
  93.7 2.9 %collective-permute-done.23 = bf16[72,512]{1,0:T(8,128)(2,1)S(1)} collective-permute-done((bf16[72,512]{1,0:T(8,128)(2,1)S(1)}, bf16[72,512]{1,0:T(8,128)(2,1)S(1)}, u32[]{:S(2)}, u32[]{:S(2)}) %collective-permute-start.23) | collective-permute-done | bytes 73760 | tf_op jit(solution)/shard_map/ppermute | solution.py:289
  97.2 2.1 %collective-permute-start.25 = (bf16[144,512]{1,0:T(8,128)(2,1)S(1)}, bf16[144,512]{1,0:T(8,128)(2,1)S(1)}, u32[]{:S(2)}, u32[]{:S(2)}) collective-permute-start(bf16[144,512]{1,0:T(8,128)(2,1)S(1)} %get-tuple-element.120), channel_id=1, source_target_pairs={{0,16},{8,24},{16,0},{24,8},{1,17},{9,25},{17,1},{25,9},{2,18},{10... | collective-permute-start | bytes 442376 | tf_op jit(solution)/shard_map/ppermute | solution.py:349
  99.2 2.8 %collective-permute-start.26 = (bf16[144,512]{1,0:T(8,128)(2,1)S(1)}, bf16[144,512]{1,0:T(8,128)(2,1)S(1)}, u32[]{:S(2)}, u32[]{:S(2)}) collective-permute-start(bf16[144,512]{1,0:T(8,128)(2,1)S(1)} %get-tuple-element.120), channel_id=1, source_target_pairs={{0,24},{8,0},{16,8},{24,16},{1,25},{9,1},{17,9},{25,17},{2,26},{10... | collective-permute-start | bytes 442376 | tf_op jit(solution)/shard_map/ppermute | solution.py:349
  104.0 1.7 %collective-permute-done.25 = bf16[144,512]{1,0:T(8,128)(2,1)S(1)} collective-permute-done((bf16[144,512]{1,0:T(8,128)(2,1)S(1)}, bf16[144,512]{1,0:T(8,128)(2,1)S(1)}, u32[]{:S(2)}, u32[]{:S(2)}) %collective-permute-start.25) | collective-permute-done | bytes 147488 | tf_op jit(solution)/shard_map/ppermute | solution.py:349
  107.1 1.6 %collective-permute-start.18 = (bf16[40,512]{1,0:T(8,128)(2,1)S(1)}, bf16[40,512]{1,0:T(8,128)(2,1)S(1)}, u32[]{:S(2)}, u32[]{:S(2)}) collective-permute-start(bf16[40,512]{1,0:T(8,128)(2,1)S(1)} %add_convert_fusion.7), channel_id=1, source_target_pairs={{0,8},{8,0},{16,24},{24,16},{1,9},{9,1},{17,25},{25,17},{2,10},{10... | collective-permute-start | bytes 122888 | tf_op jit(solution)/shard_map/ppermute | solution.py:367
  108.8 2.4 %collective-permute-done.18 = bf16[40,512]{1,0:T(8,128)(2,1)S(1)} collective-permute-done((bf16[40,512]{1,0:T(8,128)(2,1)S(1)}, bf16[40,512]{1,0:T(8,128)(2,1)S(1)}, u32[]{:S(2)}, u32[]{:S(2)}) %collective-permute-start.18) | collective-permute-done | bytes 40992 | tf_op jit(solution)/shard_map/ppermute | solution.py:367
  111.7 3.6 %collective-permute-done.19 = bf16[40,512]{1,0:T(8,128)(2,1)S(1)} collective-permute-done((bf16[40,512]{1,0:T(8,128)(2,1)S(1)}, bf16[40,512]{1,0:T(8,128)(2,1)S(1)}, u32[]{:S(2)}, u32[]{:S(2)}) %collective-permute-start.19) | collective-permute-done | bytes 40992 | tf_op jit(solution)/shard_map/ppermute | solution.py:367
  117.8 1.4 %shard_map.183 = (f32[512,512]{1,0:T(8,128)}, f32[512,512]{1,0:T(8,128)}, f32[64,512]{1,0:T(8,128)}, f32[64,64]{1,0:T(8,128)}) custom-call(bf16[1152,512]{1,0:T(8,128)(2,1)S(1)} %maximum_select_fusion.source_ref), custom_call_target="tpu_custom_call" | custom-call | flops 589824 | bytes 3424256 | tf_op jit(solution)/shard_map/pallas_call | solution.py:223
  (103 shorter events, 15.9 us)
Async XLA Ops:
  0.7 9.5 %copy-start.17 = (bf16[512,512]{1,0:T(8,128)(2,1)S(1)}, bf16[512,512]{1,0:T(8,128)(2,1)}, u32[]{:S(2)}) copy-start(bf16[512,512]{1,0:T(8,128)(2,1)} %second_ref.1) | copy-start | bytes 1572868
  4.0 6.4 %collective-permute-start.4 = (bf16[16,8192]{1,0:T(8,128)(2,1)S(1)}, bf16[16,8192]{1,0:T(8,128)(2,1)S(1)}, u32[]{:S(2)}, u32[]{:S(2)}) collective-permute-start(bf16[16,8192]{1,0:T(8,128)(2,1)S(1)} %bitcast.21), channel_id=1, source_target_pairs={{0,1},{1,0},{2,3},{3,2},{4,5},{5,4},{6,7},{7,6},{8,9},{9,8},{10,11... | collective-permute-start | bytes 786440 | tf_op jit(solution)/shard_map/ppermute | solution.py:292
  4.6 14.8 %collective-permute-start.2 = (bf16[512,256]{1,0:T(8,128)(2,1)S(1)}, bf16[512,256]{1,0:T(8,128)(2,1)}, u32[]{:S(2)}, u32[]{:S(2)}) collective-permute-start(bf16[512,256]{1,0:T(8,128)(2,1)S(1)} %get-tuple-element.63.rows_ref), channel_id=1, source_target_pairs={{0,2},{1,3},{2,0},{3,1},{4,6},{5,7},{6,4},{7,5},{8,10},{9,11},{10,... | collective-permute-start | bytes 786440 | tf_op jit(solution)/shard_map/ppermute | solution.py:283
  7.2 3.2 %collective-permute-start.3 = (s32[2,8,1,1024]{3,2,1,0:T(1,128)S(1)}, s32[2,8,1,1024]{3,2,1,0:T(1,128)S(1)}, u32[]{:S(2)}, u32[]{:S(2)}) collective-permute-start(s32[2,8,1,1024]{3,2,1,0:T(1,128)S(1)} %pad_add_fusion.refs_0_.refs_2_.refs_4_), channel_id=1, source_target_pairs={{0,1},{1,0},{2,3},{3,2},{4,5},{5,4},{6,7},{7,6},{8,9},{9,8},{10,11... | collective-permute-start | bytes 196616 | tf_op jit(solution)/shard_map/ppermute | solution.py:292
  7.4 21.3 %collective-permute-start.1 = (bf16[512,256]{1,0:T(8,128)(2,1)S(1)}, bf16[512,256]{1,0:T(8,128)(2,1)S(1)}, u32[]{:S(2)}, u32[]{:S(2)}) collective-permute-start(bf16[512,256]{1,0:T(8,128)(2,1)S(1)} %get-tuple-element.63.rows_ref), channel_id=1, source_target_pairs={{0,4},{1,5},{2,6},{3,7},{4,0},{5,1},{6,2},{7,3},{8,12},{9,13},{10,... | collective-permute-start | bytes 786440 | tf_op jit(solution)/shard_map/ppermute | solution.py:283
  10.0 20.9 %collective-permute-start = (bf16[512,256]{1,0:T(8,128)(2,1)S(1)}, bf16[512,256]{1,0:T(8,128)(2,1)S(1)}, u32[]{:S(2)}, u32[]{:S(2)}) collective-permute-start(bf16[512,256]{1,0:T(8,128)(2,1)S(1)} %get-tuple-element.63.rows_ref), channel_id=1, source_target_pairs={{0,6},{1,7},{2,4},{3,5},{4,2},{5,3},{6,0},{7,1},{8,14},{9,15},{10,... | collective-permute-start | bytes 786440 | tf_op jit(solution)/shard_map/ppermute | solution.py:283
  33.1 1.9 %collective-permute-start.5 = (f32[512,256]{1,0:T(8,128)S(1)}, f32[512,256]{1,0:T(8,128)S(1)}, u32[]{:S(2)}, u32[]{:S(2)}) collective-permute-start(f32[512,256]{1,0:T(8,128)S(1)} %get-tuple-element.78), channel_id=1, source_target_pairs={{0,1},{1,0},{2,3},{3,2},{4,5},{5,4},{6,7},{7,6},{8,9},{9,8},{10,11... | collective-permute-start | bytes 1572872 | tf_op jit(solution)/shard_map/ppermute | solution.py:292
  51.3 10.5 %collective-permute-start.7 = (bf16[576,512]{1,0:T(8,128)(2,1)}, bf16[576,512]{1,0:T(8,128)(2,1)}, u32[]{:S(2)}, u32[]{:S(2)}) collective-permute-start(bf16[576,512]{1,0:T(8,128)(2,1)} %get-tuple-element.121), channel_id=1, source_target_pairs={{0,1},{1,0},{2,3},{3,2},{4,5},{5,4},{6,7},{7,6},{8,9},{9,8},{10,11... | collective-permute-start | bytes 1769480 | tf_op jit(solution)/shard_map/ppermute | solution.py:292
  51.4 2.2 %collective-permute-start.6 = (bf16[512,256]{1,0:T(8,128)(2,1)S(1)}, bf16[512,256]{1,0:T(8,128)(2,1)S(1)}, u32[]{:S(2)}, u32[]{:S(2)}) collective-permute-start(bf16[512,256]{1,0:T(8,128)(2,1)S(1)} %get-tuple-element.100.own_ref), channel_id=1, source_target_pairs={{0,1},{1,0},{2,3},{3,2},{4,5},{5,4},{6,7},{7,6},{8,9},{9,8},{10,11... | collective-permute-start | bytes 786440 | tf_op jit(solution)/shard_map/ppermute | solution.py:292
  55.7 15.7 %collective-permute-start.11 = (bf16[512,256]{1,0:T(8,128)(2,1)S(1)}, bf16[512,256]{1,0:T(8,128)(2,1)S(1)}, u32[]{:S(2)}, u32[]{:S(2)}) collective-permute-start(bf16[512,256]{1,0:T(8,128)(2,1)S(1)} %get-tuple-element.82), channel_id=1, source_target_pairs={{0,2},{1,3},{6,4},{7,5},{8,10},{9,11},{14,12},{15,13},{16,18},{17,... | collective-permute-start | bytes 786440 | tf_op jit(solution)/shard_map/ppermute | solution.py:283
  61.1 12.8 %collective-permute-start.12 = (bf16[512,256]{1,0:T(8,128)(2,1)S(1)}, bf16[512,256]{1,0:T(8,128)(2,1)S(1)}, u32[]{:S(2)}, u32[]{:S(2)}) collective-permute-start(bf16[512,256]{1,0:T(8,128)(2,1)S(1)} %get-tuple-element.82), channel_id=1, source_target_pairs={{2,4},{3,5},{4,2},{5,3},{10,12},{11,13},{12,10},{13,11},{18,20},{1... | collective-permute-start | bytes 786440 | tf_op jit(solution)/shard_map/ppermute | solution.py:283
  63.2 10.5 %collective-permute-start.8 = (bf16[144,512]{1,0:T(8,128)(2,1)S(1)}, bf16[144,512]{1,0:T(8,128)(2,1)S(1)}, u32[]{:S(2)}, u32[]{:S(2)}) collective-permute-start(bf16[144,512]{1,0:T(8,128)(2,1)S(1)} %get-tuple-element.125), channel_id=1, source_target_pairs={{0,8},{8,16},{16,24},{24,0},{1,9},{9,17},{17,25},{25,1},{2,10},{10... | collective-permute-start | bytes 442376 | tf_op jit(solution)/shard_map/ppermute | solution.py:339
  64.7 9.0 %collective-permute-start.9 = (bf16[144,512]{1,0:T(8,128)(2,1)S(1)}, bf16[144,512]{1,0:T(8,128)(2,1)S(1)}, u32[]{:S(2)}, u32[]{:S(2)}) collective-permute-start(bf16[144,512]{1,0:T(8,128)(2,1)S(1)} %get-tuple-element.124), channel_id=1, source_target_pairs={{0,16},{8,24},{16,0},{24,8},{1,17},{9,25},{17,1},{25,9},{2,18},{10... | collective-permute-start | bytes 442376 | tf_op jit(solution)/shard_map/ppermute | solution.py:339
  66.3 7.4 %collective-permute-start.10 = (bf16[144,512]{1,0:T(8,128)(2,1)S(1)}, bf16[144,512]{1,0:T(8,128)(2,1)S(1)}, u32[]{:S(2)}, u32[]{:S(2)}) collective-permute-start(bf16[144,512]{1,0:T(8,128)(2,1)S(1)} %get-tuple-element.123), channel_id=1, source_target_pairs={{0,24},{8,0},{16,8},{24,16},{1,25},{9,1},{17,9},{25,17},{2,26},{10... | collective-permute-start | bytes 442376 | tf_op jit(solution)/shard_map/ppermute | solution.py:339
  71.4 16.7 %collective-permute-start.14 = (bf16[512,256]{1,0:T(8,128)(2,1)S(1)}, bf16[512,256]{1,0:T(8,128)(2,1)S(1)}, u32[]{:S(2)}, u32[]{:S(2)}) collective-permute-start(bf16[512,256]{1,0:T(8,128)(2,1)S(1)} %get-tuple-element.104), channel_id=1, source_target_pairs={{0,2},{1,3},{2,0},{3,1},{4,6},{5,7},{6,4},{7,5},{8,10},{9,11},{10,... | collective-permute-start | bytes 786440 | tf_op jit(solution)/shard_map/ppermute | solution.py:283
  73.9 14.6 %collective-permute-start.13 = (bf16[512,256]{1,0:T(8,128)(2,1)S(1)}, bf16[512,256]{1,0:T(8,128)(2,1)S(1)}, u32[]{:S(2)}, u32[]{:S(2)}) collective-permute-start(bf16[512,256]{1,0:T(8,128)(2,1)S(1)} %add_convert_fusion.1), channel_id=1, source_target_pairs={{0,4},{1,5},{2,6},{3,7},{4,0},{5,1},{6,2},{7,3},{8,12},{9,13},{10,... | collective-permute-start | bytes 786440 | tf_op jit(solution)/shard_map/ppermute | solution.py:283
  75.3 10.3 %collective-permute-start.21 = (bf16[72,512]{1,0:T(8,128)(2,1)S(1)}, bf16[72,512]{1,0:T(8,128)(2,1)S(1)}, u32[]{:S(2)}, u32[]{:S(2)}) collective-permute-start(bf16[72,512]{1,0:T(8,128)(2,1)S(1)} %broadcast_select_fusion.2), channel_id=1, source_target_pairs={{0,2},{1,3},{2,0},{3,1},{4,6},{5,7},{6,4},{7,5},{8,10},{9,11},{10,... | collective-permute-start | bytes 221192 | tf_op jit(solution)/shard_map/ppermute | solution.py:289
  76.4 12.1 %copy-start = (bf16[1,2048,512]{2,1,0:T(8,128)(2,1)S(1)}, bf16[1,2048,512]{2,1,0:T(8,128)(2,1)}, u32[]{:S(2)}) copy-start(bf16[1,2048,512]{2,1,0:T(8,128)(2,1)} %param.12) | copy-start | bytes 6291460
  76.4 12.1 %copy-start.1 = (bf16[2048,512]{1,0:T(8,128)(2,1)S(1)}, bf16[2048,512]{1,0:T(8,128)(2,1)}, u32[]{:S(2)}) copy-start(bf16[2048,512]{1,0:T(8,128)(2,1)} %get-tuple-element.106.refs_6_) | copy-start | bytes 6291460
  78.4 10.1 %copy-start.2 = (bf16[512,64]{0,1:T(8,128)(2,1)S(1)}, bf16[512,64]{0,1:T(8,128)(2,1)}, u32[]{:S(2)}) copy-start(bf16[512,64]{0,1:T(8,128)(2,1)} %param.18) | copy-start | bytes 196612
  85.7 5.7 %collective-permute-start.22 = (bf16[72,512]{1,0:T(8,128)(2,1)S(1)}, bf16[72,512]{1,0:T(8,128)(2,1)S(1)}, u32[]{:S(2)}, u32[]{:S(2)}) collective-permute-start(bf16[72,512]{1,0:T(8,128)(2,1)S(1)} %add_convert_fusion.4), channel_id=1, source_target_pairs={{0,4},{1,5},{2,6},{3,7},{4,0},{5,1},{6,2},{7,3},{8,12},{9,13},{10,... | collective-permute-start | bytes 221192 | tf_op jit(solution)/shard_map/ppermute | solution.py:374
  91.3 2.3 %collective-permute-start.15 = (bf16[40,512]{1,0:T(8,128)(2,1)S(1)}, bf16[40,512]{1,0:T(8,128)(2,1)S(1)}, u32[]{:S(2)}, u32[]{:S(2)}) collective-permute-start(bf16[40,512]{1,0:T(8,128)(2,1)S(1)} %broadcast_select_fusion.3), channel_id=1, source_target_pairs={{0,1},{1,0},{2,3},{3,2},{4,5},{5,4},{6,7},{7,6},{8,9},{9,8},{10,11... | collective-permute-start | bytes 122888 | tf_op jit(solution)/shard_map/ppermute | solution.py:292
  91.4 5.2 %collective-permute-start.23 = (bf16[72,512]{1,0:T(8,128)(2,1)S(1)}, bf16[72,512]{1,0:T(8,128)(2,1)S(1)}, u32[]{:S(2)}, u32[]{:S(2)}) collective-permute-start(bf16[72,512]{1,0:T(8,128)(2,1)S(1)} %add_convert_fusion.3), channel_id=1, source_target_pairs={{0,2},{1,3},{2,0},{3,1},{4,6},{5,7},{6,4},{7,5},{8,10},{9,11},{10,... | collective-permute-start | bytes 221192 | tf_op jit(solution)/shard_map/ppermute | solution.py:289
  93.6 8.5 %collective-permute-start.16 = (bf16[40,512]{1,0:T(8,128)(2,1)S(1)}, bf16[40,512]{1,0:T(8,128)(2,1)S(1)}, u32[]{:S(2)}, u32[]{:S(2)}) collective-permute-start(bf16[40,512]{1,0:T(8,128)(2,1)S(1)} %add_convert_fusion.9), channel_id=1, source_target_pairs={{0,2},{1,3},{2,0},{3,1},{4,6},{5,7},{6,4},{7,5},{8,10},{9,11},{10,... | collective-permute-start | bytes 122888 | tf_op jit(solution)/shard_map/ppermute | solution.py:374
  96.7 7.3 %collective-permute-start.24 = (bf16[144,512]{1,0:T(8,128)(2,1)S(1)}, bf16[144,512]{1,0:T(8,128)(2,1)S(1)}, u32[]{:S(2)}, u32[]{:S(2)}) collective-permute-start(bf16[144,512]{1,0:T(8,128)(2,1)S(1)} %get-tuple-element.120), channel_id=1, source_target_pairs={{0,8},{8,16},{16,24},{24,0},{1,9},{9,17},{17,25},{25,1},{2,10},{10... | collective-permute-start | bytes 442376 | tf_op jit(solution)/shard_map/ppermute | solution.py:349
  97.2 8.5 %collective-permute-start.25 = (bf16[144,512]{1,0:T(8,128)(2,1)S(1)}, bf16[144,512]{1,0:T(8,128)(2,1)S(1)}, u32[]{:S(2)}, u32[]{:S(2)}) collective-permute-start(bf16[144,512]{1,0:T(8,128)(2,1)S(1)} %get-tuple-element.120), channel_id=1, source_target_pairs={{0,16},{8,24},{16,0},{24,8},{1,17},{9,25},{17,1},{25,9},{2,18},{10... | collective-permute-start | bytes 442376 | tf_op jit(solution)/shard_map/ppermute | solution.py:349
  99.2 9.4 %collective-permute-start.26 = (bf16[144,512]{1,0:T(8,128)(2,1)S(1)}, bf16[144,512]{1,0:T(8,128)(2,1)S(1)}, u32[]{:S(2)}, u32[]{:S(2)}) collective-permute-start(bf16[144,512]{1,0:T(8,128)(2,1)S(1)} %get-tuple-element.120), channel_id=1, source_target_pairs={{0,24},{8,0},{16,8},{24,16},{1,25},{9,1},{17,9},{25,17},{2,26},{10... | collective-permute-start | bytes 442376 | tf_op jit(solution)/shard_map/ppermute | solution.py:349
  102.1 5.0 %collective-permute-start.17 = (bf16[40,512]{1,0:T(8,128)(2,1)S(1)}, bf16[40,512]{1,0:T(8,128)(2,1)S(1)}, u32[]{:S(2)}, u32[]{:S(2)}) collective-permute-start(bf16[40,512]{1,0:T(8,128)(2,1)S(1)} %add_convert_fusion.8), channel_id=1, source_target_pairs={{0,4},{1,5},{2,6},{3,7},{4,0},{5,1},{6,2},{7,3},{8,12},{9,13},{10,... | collective-permute-start | bytes 122888 | tf_op jit(solution)/shard_map/ppermute | solution.py:374
  107.1 4.1 %collective-permute-start.18 = (bf16[40,512]{1,0:T(8,128)(2,1)S(1)}, bf16[40,512]{1,0:T(8,128)(2,1)S(1)}, u32[]{:S(2)}, u32[]{:S(2)}) collective-permute-start(bf16[40,512]{1,0:T(8,128)(2,1)S(1)} %add_convert_fusion.7), channel_id=1, source_target_pairs={{0,8},{8,0},{16,24},{24,16},{1,9},{9,1},{17,25},{25,17},{2,10},{10... | collective-permute-start | bytes 122888 | tf_op jit(solution)/shard_map/ppermute | solution.py:367
  108.7 8.5 %collective-permute-start.27 = (bf16[576,512]{1,0:T(8,128)(2,1)S(1)}, bf16[576,512]{1,0:T(8,128)(2,1)S(1)}, u32[]{:S(2)}, u32[]{:S(2)}) collective-permute-start(bf16[576,512]{1,0:T(8,128)(2,1)S(1)} %constant_dynamic-update-slice_fusion), channel_id=1, source_target_pairs={{0,1},{1,0},{2,3},{3,2},{4,5},{5,4},{6,7},{7,6},{8,9},{9,8},{10,11... | collective-permute-start | bytes 1769480 | tf_op jit(solution)/shard_map/ppermute | solution.py:292
  111.2 4.1 %collective-permute-start.19 = (bf16[40,512]{1,0:T(8,128)(2,1)S(1)}, bf16[40,512]{1,0:T(8,128)(2,1)S(1)}, u32[]{:S(2)}, u32[]{:S(2)}) collective-permute-start(bf16[40,512]{1,0:T(8,128)(2,1)S(1)} %add_convert_fusion.6), channel_id=1, source_target_pairs={{0,16},{8,24},{16,0},{24,8},{1,17},{9,25},{17,1},{25,9},{2,18},{10... | collective-permute-start | bytes 122888 | tf_op jit(solution)/shard_map/ppermute | solution.py:367
  115.3 1.3 %collective-permute-start.20 = (bf16[40,512]{1,0:T(8,128)(2,1)S(1)}, bf16[40,512]{1,0:T(8,128)(2,1)S(1)}, u32[]{:S(2)}, u32[]{:S(2)}) collective-permute-start(bf16[40,512]{1,0:T(8,128)(2,1)S(1)} %add_convert_fusion.5), channel_id=1, source_target_pairs={{0,1},{1,0},{2,3},{3,2},{4,5},{5,4},{6,7},{7,6},{8,9},{9,8},{10,11... | collective-permute-start | bytes 122888 | tf_op jit(solution)/shard_map/ppermute | solution.py:292
  (16 other events, 82.9 us)
where the time goes:
time: 119 us
  Pallas kernels  41.7 us (35%)
  waiting for transfers between devices  36.7 us (31%)
  starting transfers between devices  35.1 us (29%)
  other arithmetic  3.42 us (3%)
  between operations  1.72 us (1%)
    pallas_call x13, Pallas kernels, run(): pl.pallas_call(kernel, grid=grid, in_specs=in_specs, out_specs=out_specs,...  41.7 us
    ppermute x7, starting transfers between devices, send(): return lax.ppermute(array, 'graph', pairs)  15 us
    ppermute x7, waiting for transfers between devices, send(): return lax.ppermute(array, 'graph', pairs)  13.3 us
    ppermute x2, waiting for transfers between devices, pair(): return lax.ppermute(array, 'graph', [(g, g ^ 2) for g in range(self.size)])  9.18 us
    ppermute x2, waiting for transfers between devices, summed_dp(): lax.ppermute(array, 'dp', [(g, g ^ 1 << bit) for g in range(size)])  5.98 us
    ppermute x3, starting transfers between devices, dp_joined(): other = lax.ppermute(piece, 'dp', turned(size, size, 1, turn))  5.4 us
    ppermute x3, starting transfers between devices, dp_pieces(): arrived.append(lax.ppermute(away, 'dp', turned(size, size, 1, turn)))  4.5 us
    ppermute x8, waiting for transfers between devices, swap(): return lax.ppermute(array, 'graph', [(g, g ^ 1) for g in range(self.size)])  4.19 us
  transfers between devices with their start and end apart: 28, of which 13 were waited for; matrix products, arithmetic and copies ran while one was open for 2% of the time, Pallas kernels for 16%

commit v1 on v0

--- a/solution.py
+++ b/solution.py
@@ -129,7 +129,7 @@
     pre_second = contract(first_rows, second_ref[...], 1, 0)
     logistic = sigmoid(pre_second)
     row_ids = step * tile + lax.broadcasted_iota(jnp.int32, (tile, 1), 0)
-    live = jnp.where(row_ids < count_ref[0, 0], HALF, 0.0)
+    live = jnp.where(row_ids < count_ref[0], HALF, 0.0)
     back_top = cotangent_ref[...].astype(F32) * live
     back_second = (back_top * (logistic * (1.0 + pre_second * (1.0 - logistic)))).astype(BF16)
     slope = first_logistic * (1.0 + pre_first * (1.0 - first_logistic))
@@ -147,7 +147,11 @@
 
     @pl.when(step == pl.num_programs(0) - 1)
     def _():
-        grads_ref[...] = total[...].astype(BF16)
+        rows = total.shape[0] // 2
+        core = count_ref[1]
+        for i, place in enumerate((core, 1 - core)):
+            at = pl.ds(pl.multiple_of(place * rows, 16), rows)
+            grads_ref[i * rows : (i + 1) * rows, :] = total[at, :].astype(BF16)
 
 
 def backward_kernel(count, shards_ref, own_ref, sibling_ref, *refs):
@@ -501,7 +505,7 @@
         scratch=[pltpu.VMEM((grad_rows, wide), F32)],
         grant=DENSE_GRANT,
     )(
-        edge_count,
+        jnp.stack([edge_count[0, 0], line.core.astype(jnp.int32)]),
         in_hbm(edge_rows),
         in_hbm(cotangent[0]),
         in_hbm(totals[0]) if line.groups == 1 else totals[0],
@@ -584,7 +588,9 @@
         )[0]
         return [own] + parts, basis_grad, pieces
 
-    back_parts, basis_grad, dense_grads = backward_line(0, kept, across_cores(dense_grads, line))
+    back_parts, basis_grad, dense_grads = backward_line(
+        0, kept, [dense_grads[: grad_rows // 2], line.swap(dense_grads[grad_rows // 2 :])]
+    )
     if chips > 1:
         dense_grads = add(*across_chips(dense_grads, line))
     dense_grads = summed_graph(dense_grads, line, range(2, graph_bits))

time: 119 us -> 118 us (level)
  other arithmetic: 3.42 us -> 1.26 us
  local copies, waits for them, and re-layouts: 0.65 us -> 2.58 us
where the time goes in v1:
time: 118 us
  Pallas kernels  40.8 us (35%)
  waiting for transfers between devices  36.4 us (31%)
  starting transfers between devices  35.1 us (30%)
  local copies, waits for them, and re-layouts  2.58 us (2%)
  between operations  1.7 us (1%)
  other arithmetic  1.26 us (1%)
    pallas_call x13, Pallas kernels, run(): pl.pallas_call(kernel, grid=grid, in_specs=in_specs, out_specs=out_specs,...  40.8 us
    ppermute x7, starting transfers between devices, send(): return lax.ppermute(array, 'graph', pairs)  15 us
    ppermute x7, waiting for transfers between devices, send(): return lax.ppermute(array, 'graph', pairs)  13.2 us
    ppermute x2, waiting for transfers between devices, pair(): return lax.ppermute(array, 'graph', [(g, g ^ 2) for g in range(self.size)])  9.13 us
    ppermute x2, waiting for transfers between devices, summed_dp(): lax.ppermute(array, 'dp', [(g, g ^ 1 << bit) for g in range(size)])  6.03 us
    ppermute x3, starting transfers between devices, dp_joined(): other = lax.ppermute(piece, 'dp', turned(size, size, 1, turn))  5.44 us
    ppermute x3, starting transfers between devices, dp_pieces(): arrived.append(lax.ppermute(away, 'dp', turned(size, size, 1, turn)))  4.5 us
    ppermute x8, waiting for transfers between devices, swap(): return lax.ppermute(array, 'graph', [(g, g ^ 1) for g in range(self.size)])  4.11 us
  transfers between devices with their start and end apart: 28, of which 13 were waited for; matrix products, arithmetic and copies ran while one was open for 2% of the time, Pallas kernels for 16%

profile of v1, /device:TPU:0, one launch (start us, length us, event | category | flops | bytes accessed | tf_op | source)
XLA Modules:
  0.0 117.9 jit_solution(16300860793482543027)
XLA Ops:
  0.7 3.3 %shard_map.171 = (bf16[512,256]{1,0:T(8,128)(2,1)S(1)}, f32[512,256]{1,0:T(8,128)S(1)}) custom-call(bf16[2048,512]{1,0:T(8,128)(2,1)} %bitcast.17, bf16[64,512]{1,0:T(8,128)(2,1)} %bitcast.22), custom_call_target="tpu_custom_call" | custom-call | flops 134217728 | bytes 2949120 | tf_op jit(solution)/shard_map/pallas_call | solution.py:227
  4.5 2.7 %collective-permute-start.2 = (bf16[512,256]{1,0:T(8,128)(2,1)S(1)}, bf16[512,256]{1,0:T(8,128)(2,1)S(1)}, u32[]{:S(2)}, u32[]{:S(2)}) collective-permute-start(bf16[512,256]{1,0:T(8,128)(2,1)S(1)} %get-tuple-element.63.rows_ref), channel_id=1, source_target_pairs={{0,2},{1,3},{2,0},{3,1},{4,6},{5,7},{6,4},{7,5},{8,10},{9,11},{10,... | collective-permute-start | bytes 786440 | tf_op jit(solution)/shard_map/ppermute | solution.py:287
  7.3 2.6 %collective-permute-start.1 = (bf16[512,256]{1,0:T(8,128)(2,1)S(1)}, bf16[512,256]{1,0:T(8,128)(2,1)S(1)}, u32[]{:S(2)}, u32[]{:S(2)}) collective-permute-start(bf16[512,256]{1,0:T(8,128)(2,1)S(1)} %get-tuple-element.63.rows_ref), channel_id=1, source_target_pairs={{0,4},{1,5},{2,6},{3,7},{4,0},{5,1},{6,2},{7,3},{8,12},{9,13},{10,... | collective-permute-start | bytes 786440 | tf_op jit(solution)/shard_map/ppermute | solution.py:287
  11.5 2.1 %shard_map.172 = (f32[512,256]{1,0:T(8,128)S(1)}, f32[512,256]{1,0:T(8,128)S(1)}, bf16[2,64,1024]{2,1,0:T(8,128)(2,1)}, bf16[2,64,1024]{2,1,0:T(8,128)(2,1)}) custom-call(s32[1]{0:T(128)} %bitcast.shard_ref.shards_ref, bf16[512,256]{1,0:T(8,128)(2,1)S(1)} %get-tuple-element.63.rows_ref, s32[2,8,1,1024]{3,2,1,0:T(1,128)S(1)} %pad_add_fusion.refs_0_.refs_2_.refs_4_, ...), custom_call_target="tpu_custom_call" | custom-call | flops 1073741824 | bytes 2492420 | tf_op jit(solution)/shard_map/pallas_call | solution.py:227
  13.6 5.6 %collective-permute-done.2.rows_ref = bf16[512,256]{1,0:T(8,128)(2,1)S(1)} collective-permute-done((bf16[512,256]{1,0:T(8,128)(2,1)S(1)}, bf16[512,256]{1,0:T(8,128)(2,1)S(1)}, u32[]{:S(2)}, u32[]{:S(2)}) %collective-permute-start.2) | collective-permute-done | bytes 262176 | tf_op jit(solution)/shard_map/ppermute | solution.py:287
  19.2 2.2 %shard_map.173 = (f32[512,256]{1,0:T(8,128)S(1)}, f32[512,256]{1,0:T(8,128)S(1)}, bf16[2,64,1024]{2,1,0:T(8,128)(2,1)}, bf16[2,64,1024]{2,1,0:T(8,128)(2,1)}) custom-call(s32[1]{0:T(128)} %bitcast.8.shard_ref, bf16[512,256]{1,0:T(8,128)(2,1)S(1)} %collective-permute-done.2.rows_ref, ...), custom_call_target="tpu_custom_call", output_to_operand_aliasing={{0}: (7, {}), {1}: (8, {})} | custom-call | flops 1073741824 | bytes 3540996 | tf_op jit(solution)/shard_map/pallas_call | solution.py:227
  21.3 7.3 %collective-permute-done.1.rows_ref = bf16[512,256]{1,0:T(8,128)(2,1)S(1)} collective-permute-done((bf16[512,256]{1,0:T(8,128)(2,1)S(1)}, bf16[512,256]{1,0:T(8,128)(2,1)S(1)}, u32[]{:S(2)}, u32[]{:S(2)}) %collective-permute-start.1) | collective-permute-done | bytes 262176 | tf_op jit(solution)/shard_map/ppermute | solution.py:287
  28.6 2.1 %shard_map.174 = (f32[512,256]{1,0:T(8,128)S(1)}, f32[512,256]{1,0:T(8,128)S(1)}, bf16[2,64,1024]{2,1,0:T(8,128)(2,1)}, bf16[2,64,1024]{2,1,0:T(8,128)(2,1)}) custom-call(s32[1]{0:T(128)} %bitcast.7.shard_ref, bf16[512,256]{1,0:T(8,128)(2,1)S(1)} %collective-permute-done.1.rows_ref, ...), custom_call_target="tpu_custom_call", output_to_operand_aliasing={{0}: (7, {}), {1}: (8, {})} | custom-call | flops 1073741824 | bytes 3540996 | tf_op jit(solution)/shard_map/pallas_call | solution.py:227
  30.8 2.3 %shard_map.175 = (f32[512,256]{1,0:T(8,128)}, f32[512,256]{1,0:T(8,128)S(1)}, bf16[2,64,1024]{2,1,0:T(8,128)(2,1)}, bf16[2,64,1024]{2,1,0:T(8,128)(2,1)}) custom-call(s32[1]{0:T(128)} %bitcast.5.shard_ref.shards_ref, bf16[512,256]{1,0:T(8,128)(2,1)S(1)} %collective-permute-done.rows_ref, ...), custom_call_target="tpu_custom_call", output_to_operand_aliasing={{1}: (8, {})} | custom-call | flops 1073741824 | bytes 3540996 | tf_op jit(solution)/shard_map/pallas_call | solution.py:227
  35.0 15.2 %shard_map.176 = (bf16[2048,512]{1,0:T(8,128)(2,1)}, bf16[512,256]{1,0:T(8,128)(2,1)S(1)}, bf16[1152,512]{1,0:T(8,128)(2,1)S(1)}) custom-call(s32[2]{0:T(128)S(1)} %pad_add_fusion.1.count_ref, bf16[2048,512]{1,0:T(8,128)(2,1)} %bitcast.18, bf16[2048,512]{1,0:T(8,128)(2,1)} %bitcast.32, f32[512,256]{1,0:T(8,128)} %get-tuple-element.77.gathered_ref, ...), custom_call_target="tpu_custom_call" | custom-call | flops 6845104128 | bytes 10952712 | tf_op jit(solution)/shard_map/pallas_call | solution.py:227
  51.7 1.7 %collective-permute-done.6.sibling_ref = bf16[512,256]{1,0:T(8,128)(2,1)S(1)} collective-permute-done((bf16[512,256]{1,0:T(8,128)(2,1)S(1)}, bf16[512,256]{1,0:T(8,128)(2,1)S(1)}, u32[]{:S(2)}, u32[]{:S(2)}) %collective-permute-start.6) | collective-permute-done | bytes 262176 | tf_op jit(solution)/shard_map/ppermute | solution.py:296
  53.5 2.0 %shard_map.177 = (bf16[512,256]{1,0:T(8,128)(2,1)S(1)}, bf16[2,64,1024]{2,1,0:T(8,128)(2,1)S(1)}) custom-call(s32[1]{0:T(128)} %bitcast.5.shard_ref.shards_ref, bf16[512,256]{1,0:T(8,128)(2,1)S(1)} %get-tuple-element.100.own_ref, bf16[512,256]{1,0:T(8,128)(2,1)S(1)} %collective-permute-done.6.sibling_ref, bf16[2,64,1024]{2,1,0:T(8,128)(2,1)S(1)} %copy-done.11, ...), custom_call_target="tpu_custom_call" | custom-call | flops 1073741824 | bytes 1703940 | tf_op jit(solution)/shard_map/pallas_call | solution.py:227
  55.5 5.4 %collective-permute-start.11 = (bf16[512,256]{1,0:T(8,128)(2,1)S(1)}, bf16[512,256]{1,0:T(8,128)(2,1)S(1)}, u32[]{:S(2)}, u32[]{:S(2)}) collective-permute-start(bf16[512,256]{1,0:T(8,128)(2,1)S(1)} %get-tuple-element.82), channel_id=1, source_target_pairs={{0,2},{1,3},{6,4},{7,5},{8,10},{9,11},{14,12},{15,13},{16,18},{17,... | collective-permute-start | bytes 786440 | tf_op jit(solution)/shard_map/ppermute | solution.py:287
  61.9 1.5 %collective-permute-start.8 = (bf16[144,512]{1,0:T(8,128)(2,1)S(1)}, bf16[144,512]{1,0:T(8,128)(2,1)S(1)}, u32[]{:S(2)}, u32[]{:S(2)}) collective-permute-start(bf16[144,512]{1,0:T(8,128)(2,1)S(1)} %get-tuple-element.125), channel_id=1, source_target_pairs={{0,8},{8,16},{16,24},{24,0},{1,9},{9,17},{17,25},{25,1},{2,10},{10... | collective-permute-start | bytes 442376 | tf_op jit(solution)/shard_map/ppermute | solution.py:343
  63.4 1.5 %collective-permute-start.9 = (bf16[144,512]{1,0:T(8,128)(2,1)S(1)}, bf16[144,512]{1,0:T(8,128)(2,1)S(1)}, u32[]{:S(2)}, u32[]{:S(2)}) collective-permute-start(bf16[144,512]{1,0:T(8,128)(2,1)S(1)} %get-tuple-element.124), channel_id=1, source_target_pairs={{0,16},{8,24},{16,0},{24,8},{1,17},{9,25},{17,1},{25,9},{2,18},{10... | collective-permute-start | bytes 442376 | tf_op jit(solution)/shard_map/ppermute | solution.py:343
  66.4 3.7 %shard_map.178 = (bf16[512,256]{1,0:T(8,128)(2,1)S(1)}, bf16[512,256]{1,0:T(8,128)(2,1)S(1)}, bf16[2,64,1024]{2,1,0:T(8,128)(2,1)S(1)}, bf16[2,64,1024]{2,1,0:T(8,128)(2,1)S(1)}) custom-call(s32[2]{0:T(128)S(1)} %pad_add_fusion.2.shards_ref, bf16[512,256]{1,0:T(8,128)(2,1)S(1)} %get-tuple-element.100.own_ref, ...), custom_call_target="tpu_custom_call" | custom-call | flops 2147483648 | bytes 2752520 | tf_op jit(solution)/shard_map/pallas_call | solution.py:227
  70.1 2.2 %collective-permute-start.14 = (bf16[512,256]{1,0:T(8,128)(2,1)S(1)}, bf16[512,256]{1,0:T(8,128)(2,1)S(1)}, u32[]{:S(2)}, u32[]{:S(2)}) collective-permute-start(bf16[512,256]{1,0:T(8,128)(2,1)S(1)} %get-tuple-element.104), channel_id=1, source_target_pairs={{0,2},{1,3},{2,0},{3,1},{4,6},{5,7},{6,4},{7,5},{8,10},{9,11},{10,... | collective-permute-start | bytes 786440 | tf_op jit(solution)/shard_map/ppermute | solution.py:287
  72.5 1.4 %collective-permute-start.13 = (bf16[512,256]{1,0:T(8,128)(2,1)S(1)}, bf16[512,256]{1,0:T(8,128)(2,1)S(1)}, u32[]{:S(2)}, u32[]{:S(2)}) collective-permute-start(bf16[512,256]{1,0:T(8,128)(2,1)S(1)} %add_convert_fusion.1), channel_id=1, source_target_pairs={{0,4},{1,5},{2,6},{3,7},{4,0},{5,1},{6,2},{7,3},{8,12},{9,13},{10,... | collective-permute-start | bytes 786440 | tf_op jit(solution)/shard_map/ppermute | solution.py:287
  75.0 2.0 %shard_map.179 = (bf16[512,256]{1,0:T(8,128)(2,1)S(1)}, bf16[2,64,1024]{2,1,0:T(8,128)(2,1)S(1)}) custom-call(s32[1]{0:T(128)} %bitcast.shard_ref.shards_ref, bf16[512,256]{1,0:T(8,128)(2,1)S(1)} %get-tuple-element.100.own_ref, bf16[512,256]{1,0:T(8,128)(2,1)S(1)} %collective-permute-done.6.sibling_ref, bf16[2,64,1024]{2,1,0:T(8,128)(2,1)S(1)} %copy-done.13, ...), custom_call_target="tpu_custom_call" | custom-call | flops 1073741824 | bytes 1703940 | tf_op jit(solution)/shard_map/pallas_call | solution.py:227
  78.1 6.3 %collective-permute-done.21 = bf16[72,512]{1,0:T(8,128)(2,1)S(1)} collective-permute-done((bf16[72,512]{1,0:T(8,128)(2,1)S(1)}, bf16[72,512]{1,0:T(8,128)(2,1)S(1)}, u32[]{:S(2)}, u32[]{:S(2)}) %collective-permute-start.21) | collective-permute-done | bytes 73760 | tf_op jit(solution)/shard_map/ppermute | solution.py:293
  84.4 2.4 %collective-permute-start.22 = (bf16[72,512]{1,0:T(8,128)(2,1)S(1)}, bf16[72,512]{1,0:T(8,128)(2,1)S(1)}, u32[]{:S(2)}, u32[]{:S(2)}) collective-permute-start(bf16[72,512]{1,0:T(8,128)(2,1)S(1)} %add_convert_fusion.4), channel_id=1, source_target_pairs={{0,4},{1,5},{2,6},{3,7},{4,0},{5,1},{6,2},{7,3},{8,12},{9,13},{10,... | collective-permute-start | bytes 221192 | tf_op jit(solution)/shard_map/ppermute | solution.py:378
  87.1 2.8 %shard_map.181 = (bf16[2048,512]{1,0:T(8,128)(2,1)}, bf16[80,512]{1,0:T(8,128)(2,1)S(1)}) custom-call(bf16[512,256]{1,0:T(8,128)(2,1)S(1)} %get-tuple-element.103.refs_0_, bf16[512,256]{1,0:T(8,128)(2,1)S(1)} %collective-permute-done.12.refs_1_, bf16[512,256]{1,0:T(8,128)(2,1)S(1)} %collective-permute-done.13.refs_2_, ...), custom_call_target="tpu_custom_call" | custom-call | flops 268435456 | bytes 8015872 | tf_op jit(solution)/shard_map/pallas_call | solution.py:227
  90.1 2.2 %collective-permute-start.23 = (bf16[72,512]{1,0:T(8,128)(2,1)S(1)}, bf16[72,512]{1,0:T(8,128)(2,1)S(1)}, u32[]{:S(2)}, u32[]{:S(2)}) collective-permute-start(bf16[72,512]{1,0:T(8,128)(2,1)S(1)} %add_convert_fusion.3), channel_id=1, source_target_pairs={{0,2},{1,3},{2,0},{3,1},{4,6},{5,7},{6,4},{7,5},{8,10},{9,11},{10,... | collective-permute-start | bytes 221192 | tf_op jit(solution)/shard_map/ppermute | solution.py:293
  92.4 2.8 %collective-permute-done.23 = bf16[72,512]{1,0:T(8,128)(2,1)S(1)} collective-permute-done((bf16[72,512]{1,0:T(8,128)(2,1)S(1)}, bf16[72,512]{1,0:T(8,128)(2,1)S(1)}, u32[]{:S(2)}, u32[]{:S(2)}) %collective-permute-start.23) | collective-permute-done | bytes 73760 | tf_op jit(solution)/shard_map/ppermute | solution.py:293
  95.8 2.1 %collective-permute-start.25 = (bf16[144,512]{1,0:T(8,128)(2,1)S(1)}, bf16[144,512]{1,0:T(8,128)(2,1)S(1)}, u32[]{:S(2)}, u32[]{:S(2)}) collective-permute-start(bf16[144,512]{1,0:T(8,128)(2,1)S(1)} %get-tuple-element.120), channel_id=1, source_target_pairs={{0,16},{8,24},{16,0},{24,8},{1,17},{9,25},{17,1},{25,9},{2,18},{10... | collective-permute-start | bytes 442376 | tf_op jit(solution)/shard_map/ppermute | solution.py:353
  97.9 2.8 %collective-permute-start.26 = (bf16[144,512]{1,0:T(8,128)(2,1)S(1)}, bf16[144,512]{1,0:T(8,128)(2,1)S(1)}, u32[]{:S(2)}, u32[]{:S(2)}) collective-permute-start(bf16[144,512]{1,0:T(8,128)(2,1)S(1)} %get-tuple-element.120), channel_id=1, source_target_pairs={{0,24},{8,0},{16,8},{24,16},{1,25},{9,1},{17,9},{25,17},{2,26},{10... | collective-permute-start | bytes 442376 | tf_op jit(solution)/shard_map/ppermute | solution.py:353
  102.6 1.7 %collective-permute-done.25 = bf16[144,512]{1,0:T(8,128)(2,1)S(1)} collective-permute-done((bf16[144,512]{1,0:T(8,128)(2,1)S(1)}, bf16[144,512]{1,0:T(8,128)(2,1)S(1)}, u32[]{:S(2)}, u32[]{:S(2)}) %collective-permute-start.25) | collective-permute-done | bytes 147488 | tf_op jit(solution)/shard_map/ppermute | solution.py:353
  104.3 1.5 %collective-permute-done.17 = bf16[40,512]{1,0:T(8,128)(2,1)S(1)} collective-permute-done((bf16[40,512]{1,0:T(8,128)(2,1)S(1)}, bf16[40,512]{1,0:T(8,128)(2,1)S(1)}, u32[]{:S(2)}, u32[]{:S(2)}) %collective-permute-start.17) | collective-permute-done | bytes 40992 | tf_op jit(solution)/shard_map/ppermute | solution.py:378
  105.8 1.6 %collective-permute-start.18 = (bf16[40,512]{1,0:T(8,128)(2,1)S(1)}, bf16[40,512]{1,0:T(8,128)(2,1)S(1)}, u32[]{:S(2)}, u32[]{:S(2)}) collective-permute-start(bf16[40,512]{1,0:T(8,128)(2,1)S(1)} %add_convert_fusion.7), channel_id=1, source_target_pairs={{0,8},{8,0},{16,24},{24,16},{1,9},{9,1},{17,25},{25,17},{2,10},{10... | collective-permute-start | bytes 122888 | tf_op jit(solution)/shard_map/ppermute | solution.py:371
  107.5 2.4 %collective-permute-done.18 = bf16[40,512]{1,0:T(8,128)(2,1)S(1)} collective-permute-done((bf16[40,512]{1,0:T(8,128)(2,1)S(1)}, bf16[40,512]{1,0:T(8,128)(2,1)S(1)}, u32[]{:S(2)}, u32[]{:S(2)}) %collective-permute-start.18) | collective-permute-done | bytes 40992 | tf_op jit(solution)/shard_map/ppermute | solution.py:371
  110.3 3.6 %collective-permute-done.19 = bf16[40,512]{1,0:T(8,128)(2,1)S(1)} collective-permute-done((bf16[40,512]{1,0:T(8,128)(2,1)S(1)}, bf16[40,512]{1,0:T(8,128)(2,1)S(1)}, u32[]{:S(2)}, u32[]{:S(2)}) %collective-permute-start.19) | collective-permute-done | bytes 40992 | tf_op jit(solution)/shard_map/ppermute | solution.py:371
  116.5 1.4 %shard_map.183 = (f32[512,512]{1,0:T(8,128)}, f32[512,512]{1,0:T(8,128)}, f32[64,512]{1,0:T(8,128)}, f32[64,64]{1,0:T(8,128)}) custom-call(bf16[1152,512]{1,0:T(8,128)(2,1)S(1)} %maximum_select_fusion.source_ref), custom_call_target="tpu_custom_call" | custom-call | flops 589824 | bytes 3424256 | tf_op jit(solution)/shard_map/pallas_call | solution.py:227
  (102 shorter events, 15.5 us)
Async XLA Ops:
  0.7 9.3 %copy-start.16 = (bf16[512,512]{1,0:T(8,128)(2,1)S(1)}, bf16[512,512]{1,0:T(8,128)(2,1)}, u32[]{:S(2)}) copy-start(bf16[512,512]{1,0:T(8,128)(2,1)} %first_ref.1) | copy-start | bytes 1572868
  4.0 7.5 %collective-permute-start.4 = (bf16[16,8192]{1,0:T(8,128)(2,1)S(1)}, bf16[16,8192]{1,0:T(8,128)(2,1)S(1)}, u32[]{:S(2)}, u32[]{:S(2)}) collective-permute-start(bf16[16,8192]{1,0:T(8,128)(2,1)S(1)} %bitcast.24), channel_id=1, source_target_pairs={{0,1},{1,0},{2,3},{3,2},{4,5},{5,4},{6,7},{7,6},{8,9},{9,8},{10,11... | collective-permute-start | bytes 786440 | tf_op jit(solution)/shard_map/ppermute | solution.py:296
  4.5 14.7 %collective-permute-start.2 = (bf16[512,256]{1,0:T(8,128)(2,1)S(1)}, bf16[512,256]{1,0:T(8,128)(2,1)S(1)}, u32[]{:S(2)}, u32[]{:S(2)}) collective-permute-start(bf16[512,256]{1,0:T(8,128)(2,1)S(1)} %get-tuple-element.63.rows_ref), channel_id=1, source_target_pairs={{0,2},{1,3},{2,0},{3,1},{4,6},{5,7},{6,4},{7,5},{8,10},{9,11},{10,... | collective-permute-start | bytes 786440 | tf_op jit(solution)/shard_map/ppermute | solution.py:287
  7.2 4.3 %collective-permute-start.3 = (s32[2,8,1,1024]{3,2,1,0:T(1,128)S(1)}, s32[2,8,1,1024]{3,2,1,0:T(1,128)S(1)}, u32[]{:S(2)}, u32[]{:S(2)}) collective-permute-start(s32[2,8,1,1024]{3,2,1,0:T(1,128)S(1)} %pad_add_fusion.refs_0_.refs_2_.refs_4_), channel_id=1, source_target_pairs={{0,1},{1,0},{2,3},{3,2},{4,5},{5,4},{6,7},{7,6},{8,9},{9,8},{10,11... | collective-permute-start | bytes 196616 | tf_op jit(solution)/shard_map/ppermute | solution.py:296
  7.3 21.3 %collective-permute-start.1 = (bf16[512,256]{1,0:T(8,128)(2,1)S(1)}, bf16[512,256]{1,0:T(8,128)(2,1)S(1)}, u32[]{:S(2)}, u32[]{:S(2)}) collective-permute-start(bf16[512,256]{1,0:T(8,128)(2,1)S(1)} %get-tuple-element.63.rows_ref), channel_id=1, source_target_pairs={{0,4},{1,5},{2,6},{3,7},{4,0},{5,1},{6,2},{7,3},{8,12},{9,13},{10,... | collective-permute-start | bytes 786440 | tf_op jit(solution)/shard_map/ppermute | solution.py:287
  9.9 20.9 %collective-permute-start = (bf16[512,256]{1,0:T(8,128)(2,1)S(1)}, bf16[512,256]{1,0:T(8,128)(2,1)S(1)}, u32[]{:S(2)}, u32[]{:S(2)}) collective-permute-start(bf16[512,256]{1,0:T(8,128)(2,1)S(1)} %get-tuple-element.63.rows_ref), channel_id=1, source_target_pairs={{0,6},{1,7},{2,4},{3,5},{4,2},{5,3},{6,0},{7,1},{8,14},{9,15},{10,... | collective-permute-start | bytes 786440 | tf_op jit(solution)/shard_map/ppermute | solution.py:287
  33.1 1.9 %collective-permute-start.5 = (f32[512,256]{1,0:T(8,128)S(1)}, f32[512,256]{1,0:T(8,128)S(1)}, u32[]{:S(2)}, u32[]{:S(2)}) collective-permute-start(f32[512,256]{1,0:T(8,128)S(1)} %get-tuple-element.78), channel_id=1, source_target_pairs={{0,1},{1,0},{2,3},{3,2},{4,5},{5,4},{6,7},{7,6},{8,9},{9,8},{10,11... | collective-permute-start | bytes 1572872 | tf_op jit(solution)/shard_map/ppermute | solution.py:296
  51.1 10.5 %collective-permute-start.7 = (bf16[576,512]{1,0:T(8,128)(2,1)S(1)}, bf16[576,512]{1,0:T(8,128)(2,1)S(1)}, u32[]{:S(2)}, u32[]{:S(2)}) collective-permute-start(bf16[576,512]{1,0:T(8,128)(2,1)S(1)} %get-tuple-element.121), channel_id=1, source_target_pairs={{0,1},{1,0},{2,3},{3,2},{4,5},{5,4},{6,7},{7,6},{8,9},{9,8},{10,11... | collective-permute-start | bytes 1769480 | tf_op jit(solution)/shard_map/ppermute | solution.py:296
  51.2 2.2 %collective-permute-start.6 = (bf16[512,256]{1,0:T(8,128)(2,1)S(1)}, bf16[512,256]{1,0:T(8,128)(2,1)S(1)}, u32[]{:S(2)}, u32[]{:S(2)}) collective-permute-start(bf16[512,256]{1,0:T(8,128)(2,1)S(1)} %get-tuple-element.100.own_ref), channel_id=1, source_target_pairs={{0,1},{1,0},{2,3},{3,2},{4,5},{5,4},{6,7},{7,6},{8,9},{9,8},{10,11... | collective-permute-start | bytes 786440 | tf_op jit(solution)/shard_map/ppermute | solution.py:296
  55.5 14.6 %collective-permute-start.11 = (bf16[512,256]{1,0:T(8,128)(2,1)S(1)}, bf16[512,256]{1,0:T(8,128)(2,1)S(1)}, u32[]{:S(2)}, u32[]{:S(2)}) collective-permute-start(bf16[512,256]{1,0:T(8,128)(2,1)S(1)} %get-tuple-element.82), channel_id=1, source_target_pairs={{0,2},{1,3},{6,4},{7,5},{8,10},{9,11},{14,12},{15,13},{16,18},{17,... | collective-permute-start | bytes 786440 | tf_op jit(solution)/shard_map/ppermute | solution.py:287
  60.9 11.6 %collective-permute-start.12 = (bf16[512,256]{1,0:T(8,128)(2,1)S(1)}, bf16[512,256]{1,0:T(8,128)(2,1)S(1)}, u32[]{:S(2)}, u32[]{:S(2)}) collective-permute-start(bf16[512,256]{1,0:T(8,128)(2,1)S(1)} %get-tuple-element.82), channel_id=1, source_target_pairs={{2,4},{3,5},{4,2},{5,3},{10,12},{11,13},{12,10},{13,11},{18,20},{1... | collective-permute-start | bytes 786440 | tf_op jit(solution)/shard_map/ppermute | solution.py:287
  61.9 10.5 %collective-permute-start.8 = (bf16[144,512]{1,0:T(8,128)(2,1)S(1)}, bf16[144,512]{1,0:T(8,128)(2,1)S(1)}, u32[]{:S(2)}, u32[]{:S(2)}) collective-permute-start(bf16[144,512]{1,0:T(8,128)(2,1)S(1)} %get-tuple-element.125), channel_id=1, source_target_pairs={{0,8},{8,16},{16,24},{24,0},{1,9},{9,17},{17,25},{25,1},{2,10},{10... | collective-permute-start | bytes 442376 | tf_op jit(solution)/shard_map/ppermute | solution.py:343
  63.4 9.0 %collective-permute-start.9 = (bf16[144,512]{1,0:T(8,128)(2,1)S(1)}, bf16[144,512]{1,0:T(8,128)(2,1)S(1)}, u32[]{:S(2)}, u32[]{:S(2)}) collective-permute-start(bf16[144,512]{1,0:T(8,128)(2,1)S(1)} %get-tuple-element.124), channel_id=1, source_target_pairs={{0,16},{8,24},{16,0},{24,8},{1,17},{9,25},{17,1},{25,9},{2,18},{10... | collective-permute-start | bytes 442376 | tf_op jit(solution)/shard_map/ppermute | solution.py:343
  64.9 7.4 %collective-permute-start.10 = (bf16[144,512]{1,0:T(8,128)(2,1)S(1)}, bf16[144,512]{1,0:T(8,128)(2,1)S(1)}, u32[]{:S(2)}, u32[]{:S(2)}) collective-permute-start(bf16[144,512]{1,0:T(8,128)(2,1)S(1)} %get-tuple-element.123), channel_id=1, source_target_pairs={{0,24},{8,0},{16,8},{24,16},{1,25},{9,1},{17,9},{25,17},{2,26},{10... | collective-permute-start | bytes 442376 | tf_op jit(solution)/shard_map/ppermute | solution.py:343
  70.1 16.7 %collective-permute-start.14 = (bf16[512,256]{1,0:T(8,128)(2,1)S(1)}, bf16[512,256]{1,0:T(8,128)(2,1)S(1)}, u32[]{:S(2)}, u32[]{:S(2)}) collective-permute-start(bf16[512,256]{1,0:T(8,128)(2,1)S(1)} %get-tuple-element.104), channel_id=1, source_target_pairs={{0,2},{1,3},{2,0},{3,1},{4,6},{5,7},{6,4},{7,5},{8,10},{9,11},{10,... | collective-permute-start | bytes 786440 | tf_op jit(solution)/shard_map/ppermute | solution.py:287
  72.5 14.6 %collective-permute-start.13 = (bf16[512,256]{1,0:T(8,128)(2,1)S(1)}, bf16[512,256]{1,0:T(8,128)(2,1)S(1)}, u32[]{:S(2)}, u32[]{:S(2)}) collective-permute-start(bf16[512,256]{1,0:T(8,128)(2,1)S(1)} %add_convert_fusion.1), channel_id=1, source_target_pairs={{0,4},{1,5},{2,6},{3,7},{4,0},{5,1},{6,2},{7,3},{8,12},{9,13},{10,... | collective-permute-start | bytes 786440 | tf_op jit(solution)/shard_map/ppermute | solution.py:287
  74.0 10.4 %collective-permute-start.21 = (bf16[72,512]{1,0:T(8,128)(2,1)S(1)}, bf16[72,512]{1,0:T(8,128)(2,1)S(1)}, u32[]{:S(2)}, u32[]{:S(2)}) collective-permute-start(bf16[72,512]{1,0:T(8,128)(2,1)S(1)} %broadcast_select_fusion), channel_id=1, source_target_pairs={{0,2},{1,3},{2,0},{3,1},{4,6},{5,7},{6,4},{7,5},{8,10},{9,11},{10,... | collective-permute-start | bytes 221192 | tf_op jit(solution)/shard_map/ppermute | solution.py:293
  75.0 12.1 %copy-start = (bf16[1,2048,512]{2,1,0:T(8,128)(2,1)S(1)}, bf16[1,2048,512]{2,1,0:T(8,128)(2,1)}, u32[]{:S(2)}) copy-start(bf16[1,2048,512]{2,1,0:T(8,128)(2,1)} %param.12) | copy-start | bytes 6291460
  75.0 12.1 %copy-start.1 = (bf16[2048,512]{1,0:T(8,128)(2,1)S(1)}, bf16[2048,512]{1,0:T(8,128)(2,1)}, u32[]{:S(2)}) copy-start(bf16[2048,512]{1,0:T(8,128)(2,1)} %get-tuple-element.106.refs_6_) | copy-start | bytes 6291460
  77.1 10.0 %copy-start.2 = (bf16[512,64]{0,1:T(8,128)(2,1)S(1)}, bf16[512,64]{0,1:T(8,128)(2,1)}, u32[]{:S(2)}) copy-start(bf16[512,64]{0,1:T(8,128)(2,1)} %param.18) | copy-start | bytes 196612
  84.4 5.6 %collective-permute-start.22 = (bf16[72,512]{1,0:T(8,128)(2,1)S(1)}, bf16[72,512]{1,0:T(8,128)(2,1)S(1)}, u32[]{:S(2)}, u32[]{:S(2)}) collective-permute-start(bf16[72,512]{1,0:T(8,128)(2,1)S(1)} %add_convert_fusion.4), channel_id=1, source_target_pairs={{0,4},{1,5},{2,6},{3,7},{4,0},{5,1},{6,2},{7,3},{8,12},{9,13},{10,... | collective-permute-start | bytes 221192 | tf_op jit(solution)/shard_map/ppermute | solution.py:378
  90.0 2.3 %collective-permute-start.15 = (bf16[40,512]{1,0:T(8,128)(2,1)S(1)}, bf16[40,512]{1,0:T(8,128)(2,1)S(1)}, u32[]{:S(2)}, u32[]{:S(2)}) collective-permute-start(bf16[40,512]{1,0:T(8,128)(2,1)S(1)} %broadcast_select_fusion.1), channel_id=1, source_target_pairs={{0,1},{1,0},{2,3},{3,2},{4,5},{5,4},{6,7},{7,6},{8,9},{9,8},{10,11... | collective-permute-start | bytes 122888 | tf_op jit(solution)/shard_map/ppermute | solution.py:296
  90.1 5.2 %collective-permute-start.23 = (bf16[72,512]{1,0:T(8,128)(2,1)S(1)}, bf16[72,512]{1,0:T(8,128)(2,1)S(1)}, u32[]{:S(2)}, u32[]{:S(2)}) collective-permute-start(bf16[72,512]{1,0:T(8,128)(2,1)S(1)} %add_convert_fusion.3), channel_id=1, source_target_pairs={{0,2},{1,3},{2,0},{3,1},{4,6},{5,7},{6,4},{7,5},{8,10},{9,11},{10,... | collective-permute-start | bytes 221192 | tf_op jit(solution)/shard_map/ppermute | solution.py:293
  92.3 8.5 %collective-permute-start.16 = (bf16[40,512]{1,0:T(8,128)(2,1)S(1)}, bf16[40,512]{1,0:T(8,128)(2,1)S(1)}, u32[]{:S(2)}, u32[]{:S(2)}) collective-permute-start(bf16[40,512]{1,0:T(8,128)(2,1)S(1)} %add_convert_fusion.9), channel_id=1, source_target_pairs={{0,2},{1,3},{2,0},{3,1},{4,6},{5,7},{6,4},{7,5},{8,10},{9,11},{10,... | collective-permute-start | bytes 122888 | tf_op jit(solution)/shard_map/ppermute | solution.py:378
  95.3 7.2 %collective-permute-start.24 = (bf16[144,512]{1,0:T(8,128)(2,1)S(1)}, bf16[144,512]{1,0:T(8,128)(2,1)S(1)}, u32[]{:S(2)}, u32[]{:S(2)}) collective-permute-start(bf16[144,512]{1,0:T(8,128)(2,1)S(1)} %get-tuple-element.120), channel_id=1, source_target_pairs={{0,8},{8,16},{16,24},{24,0},{1,9},{9,17},{17,25},{25,1},{2,10},{10... | collective-permute-start | bytes 442376 | tf_op jit(solution)/shard_map/ppermute | solution.py:353
  95.8 8.5 %collective-permute-start.25 = (bf16[144,512]{1,0:T(8,128)(2,1)S(1)}, bf16[144,512]{1,0:T(8,128)(2,1)S(1)}, u32[]{:S(2)}, u32[]{:S(2)}) collective-permute-start(bf16[144,512]{1,0:T(8,128)(2,1)S(1)} %get-tuple-element.120), channel_id=1, source_target_pairs={{0,16},{8,24},{16,0},{24,8},{1,17},{9,25},{17,1},{25,9},{2,18},{10... | collective-permute-start | bytes 442376 | tf_op jit(solution)/shard_map/ppermute | solution.py:353
  97.9 9.4 %collective-permute-start.26 = (bf16[144,512]{1,0:T(8,128)(2,1)S(1)}, bf16[144,512]{1,0:T(8,128)(2,1)S(1)}, u32[]{:S(2)}, u32[]{:S(2)}) collective-permute-start(bf16[144,512]{1,0:T(8,128)(2,1)S(1)} %get-tuple-element.120), channel_id=1, source_target_pairs={{0,24},{8,0},{16,8},{24,16},{1,25},{9,1},{17,9},{25,17},{2,26},{10... | collective-permute-start | bytes 442376 | tf_op jit(solution)/shard_map/ppermute | solution.py:353
  100.8 5.0 %collective-permute-start.17 = (bf16[40,512]{1,0:T(8,128)(2,1)S(1)}, bf16[40,512]{1,0:T(8,128)(2,1)S(1)}, u32[]{:S(2)}, u32[]{:S(2)}) collective-permute-start(bf16[40,512]{1,0:T(8,128)(2,1)S(1)} %add_convert_fusion.8), channel_id=1, source_target_pairs={{0,4},{1,5},{2,6},{3,7},{4,0},{5,1},{6,2},{7,3},{8,12},{9,13},{10,... | collective-permute-start | bytes 122888 | tf_op jit(solution)/shard_map/ppermute | solution.py:378
  105.8 4.1 %collective-permute-start.18 = (bf16[40,512]{1,0:T(8,128)(2,1)S(1)}, bf16[40,512]{1,0:T(8,128)(2,1)S(1)}, u32[]{:S(2)}, u32[]{:S(2)}) collective-permute-start(bf16[40,512]{1,0:T(8,128)(2,1)S(1)} %add_convert_fusion.7), channel_id=1, source_target_pairs={{0,8},{8,0},{16,24},{24,16},{1,9},{9,1},{17,25},{25,17},{2,10},{10... | collective-permute-start | bytes 122888 | tf_op jit(solution)/shard_map/ppermute | solution.py:371
  107.4 8.6 %collective-permute-start.27 = (bf16[576,512]{1,0:T(8,128)(2,1)S(1)}, bf16[576,512]{1,0:T(8,128)(2,1)S(1)}, u32[]{:S(2)}, u32[]{:S(2)}) collective-permute-start(bf16[576,512]{1,0:T(8,128)(2,1)S(1)} %constant_dynamic-update-slice_fusion), channel_id=1, source_target_pairs={{0,1},{1,0},{2,3},{3,2},{4,5},{5,4},{6,7},{7,6},{8,9},{9,8},{10,11... | collective-permute-start | bytes 1769480 | tf_op jit(solution)/shard_map/ppermute | solution.py:296
  109.9 4.1 %collective-permute-start.19 = (bf16[40,512]{1,0:T(8,128)(2,1)S(1)}, bf16[40,512]{1,0:T(8,128)(2,1)S(1)}, u32[]{:S(2)}, u32[]{:S(2)}) collective-permute-start(bf16[40,512]{1,0:T(8,128)(2,1)S(1)} %add_convert_fusion.6), channel_id=1, source_target_pairs={{0,16},{8,24},{16,0},{24,8},{1,17},{9,25},{17,1},{25,9},{2,18},{10... | collective-permute-start | bytes 122888 | tf_op jit(solution)/shard_map/ppermute | solution.py:371
  114.0 1.3 %collective-permute-start.20 = (bf16[40,512]{1,0:T(8,128)(2,1)S(1)}, bf16[40,512]{1,0:T(8,128)(2,1)S(1)}, u32[]{:S(2)}, u32[]{:S(2)}) collective-permute-start(bf16[40,512]{1,0:T(8,128)(2,1)S(1)} %add_convert_fusion.5), channel_id=1, source_target_pairs={{0,1},{1,0},{2,3},{3,2},{4,5},{5,4},{6,7},{7,6},{8,9},{9,8},{10,11... | collective-permute-start | bytes 122888 | tf_op jit(solution)/shard_map/ppermute | solution.py:296
  (15 other events, 69.4 us)
